TPU v7x, 32 devices: a whole 2x2x4 slice. The times are simulated.
32 devices in a mesh: stream: 2 (over y), span: 4 (over z), vert: 4 (over x, core).
Axes of the slice: x: 2, y: 2, z: 4, core: 2. Of those that a mesh axis runs over, the one named last changes fastest.
Arguments:
- fields: float32 [5, 128, 64, 256], P(None, 'vert', 'span', 'stream'), may hold values from -6 to 6
- solid_frac: float32 [128, 64, 256], P('vert', 'span', 'stream'), may hold values from 0 to 1
- panels: float32 [512, 5, 256], P(('stream', 'span', 'vert')), may hold values from -0.0625 to 0.0625
- panel_owner: int32 [512, 1], P(('stream', 'span', 'vert')), may hold values from 0 to 15; in each aligned block of 16 rows (0 to 15, 16 to 31, ...) at most 2 rows name the same one
- deck_cells: int32 [4, 4, 2, 2048], P('vert', 'span', 'stream'), may hold values from 0 to 65535
- deck_geom: float32 [4, 4, 2, 3, 2048], P('vert', None, 'stream'), may hold values from -6 to 6
- strip_ids: int32 [4, 4, 2, 2048], P('vert', None, 'stream'), may hold values from 0 to 15, as said below
- mode_shapes: float32 [3, 16, 32], replicated, may hold values from -0.013671875 to 0.013671875
Outputs:
- new_fields: float32 [5, 128, 64, 256], P(None, 'vert', 'span', 'stream')
- modal_force: float32 [32], replicated
Inputs may be any that keep to these rules, and one draw needn't show every extreme that they name: `panel_owner`: tile number s * 4 + v for along-deck tile s and vertical tile v. Among the 16 panels of one device no tile is named more than 2 times; some device names some tile exactly 2 times. `strip_ids`: cells of along-deck tile s belong to strips s * 4 to (s + 1) * 4 - 1.
All inputs are finite; a program needn't handle non-finite values.
Results may differ from a plain program's by a relative error of at most 0.00012.
Values sent between devices are 32-bit elements; how exact they have to be, the bound alone decides.
A program may use at most 128 MiB of HBM per device.

v0:
```python
import math

import jax
import jax.numpy as jnp
from jax import lax
from jax.sharding import PartitionSpec as P

CAP = 2


time_step = 0.15
viscous = 0.05
heat_diff = 0.03
sound_sq = 1.0
buoyant = 0.5
penalty = 0.5
relax_time = 0.5
relax_depth = 8.0
wave_cols = 16


def extended(block, sides, width):
    for axis, dim in sides:
        count = lax.axis_size(axis)
        forward = [(i, i + 1) for i in range(count - 1)]
        backward = [(target, source) for source, target in forward]
        low = lax.ppermute(
            lax.slice_in_dim(block, block.shape[dim] - width, None, axis=dim), axis, forward
        )
        high = lax.ppermute(lax.slice_in_dim(block, 0, width, axis=dim), axis, backward)
        block = jnp.concatenate([low, block, high], axis=dim)
    return block


def wave_basis(heights, widths, total_z, total_y, spec):
    modes = jnp.arange(spec, dtype=jnp.int32)
    across = (modes % wave_cols)[:, None, None]
    upward = (modes // wave_cols)[:, None, None]
    period = total_y * total_z
    phase = (
        across * widths[None, None, :] * total_z + upward * heights[None, :, None] * total_y
    ) % period
    angle = phase.astype(jnp.float32) * (2.0 * math.pi / period)
    return jnp.concatenate([jnp.cos(angle), jnp.sin(angle)], axis=0)


def relax_weights(positions, limit):
    spots = positions.astype(jnp.float32)
    return jnp.where(positions < limit, jnp.exp(-spots / relax_depth) / relax_time, 0.0)


def rates(padded, solid_frac, relax_rate, target_plane):
    centre = padded[:, 1:-1, 1:-1, 1:-1]
    east_side = padded[:, 1:-1, 1:-1, 2:]
    west_side = padded[:, 1:-1, 1:-1, :-2]
    north_side = padded[:, 1:-1, 2:, 1:-1]
    south_side = padded[:, 1:-1, :-2, 1:-1]
    upper_side = padded[:, 2:, 1:-1, 1:-1]
    lower_side = padded[:, :-2, 1:-1, 1:-1]
    grad_x = 0.5 * (east_side - west_side)
    grad_y = 0.5 * (north_side - south_side)
    grad_z = 0.5 * (upper_side - lower_side)
    laplace = (
        east_side + west_side + north_side + south_side + upper_side + lower_side - 6.0 * centre
    )
    speed_x = centre[0]
    speed_y = centre[1]
    speed_z = centre[2]
    carried = speed_x * grad_x + speed_y * grad_y + speed_z * grad_z
    coeffs = jnp.array([viscous, viscous, viscous, viscous, heat_diff], jnp.float32)[
        :, None, None, None
    ]
    damping = solid_frac / penalty
    nudging = relax_rate[None, None, None, :] * (target_plane[:, :, :, None] - centre)
    common = coeffs * laplace - carried + nudging
    extra_terms = jnp.stack(
        [
            -grad_x[3] - damping * speed_x,
            -grad_y[3] - damping * speed_y,
            -grad_z[3] - damping * speed_z + buoyant * centre[4],
            -sound_sq * (grad_x[0] + grad_y[1] + grad_z[2]),
            jnp.zeros_like(speed_x),
        ]
    )
    return common + extra_terms


def pack_slots(flat_panels, target_tile, chosen, tile_count):
    running = jnp.cumsum(chosen, axis=0) - 1
    slot_rank = jnp.sum(chosen * running, axis=1)
    slot_index = target_tile * CAP + slot_rank
    dispatch = (
        slot_index[None, :] == jnp.arange(tile_count * CAP, dtype=jnp.int32)[:, None]
    ).astype(jnp.float32)
    return jnp.dot(dispatch, flat_panels, precision=lax.Precision.HIGHEST)


def strip_forces(traction, labels, strip_count):
    columns = jnp.arange(strip_count, dtype=jnp.int32)

    def add_row(running, item_pair):
        row_values, row_labels = item_pair
        member = (row_labels[:, None] == columns[None, :]).astype(jnp.float32)
        return (running + jnp.dot(row_values, member, precision=lax.Precision.HIGHEST), None)

    start_value = jnp.zeros((traction.shape[1], strip_count), jnp.float32)
    summed, ignored = lax.scan(add_row, start_value, (traction, labels))
    return summed


def on_device(
    fields, solid_frac, panels, panel_owner, deck_cells, deck_geom, strip_ids, mode_shapes
):
    depth_cells = fields.shape[1]
    span_cells = fields.shape[2]
    wind_cells = fields.shape[3]
    n_span = lax.axis_size("span")
    n_vert = lax.axis_size("vert")
    stream_pos = lax.axis_index("stream")
    span_pos = lax.axis_index("span")
    vert_pos = lax.axis_index("vert")
    tile_count = n_span * n_vert
    held_panels = panels.shape[0]
    spec_cols = panels.shape[2]
    flat_panels = panels.reshape(held_panels, 5 * spec_cols)
    target_tile = panel_owner[:, 0]
    chosen = (target_tile[:, None] == jnp.arange(tile_count, dtype=jnp.int32)[None, :]).astype(
        jnp.int32
    )
    outgoing = pack_slots(flat_panels, target_tile, chosen, tile_count)
    arrived = lax.all_to_all(
        outgoing.reshape(tile_count, CAP * 5 * spec_cols),
        ("span", "vert"),
        split_axis=0,
        concat_axis=0,
        tiled=True,
    )
    coeffs = jnp.sum(arrived.reshape(-1, 5 * spec_cols), axis=0)
    coeffs = coeffs.reshape(5, spec_cols)
    heights = vert_pos * depth_cells + jnp.arange(depth_cells, dtype=jnp.int32)
    widths = span_pos * span_cells + jnp.arange(span_cells, dtype=jnp.int32)
    wave_table = wave_basis(
        heights, widths, depth_cells * n_vert, span_cells * n_span, spec_cols // 2
    )
    wave_table = wave_table.reshape(spec_cols, depth_cells * span_cells)
    partial_value = jnp.dot(coeffs, wave_table, precision=lax.Precision.HIGHEST)
    inflow_plane = lax.psum(partial_value, "stream").reshape(5, depth_cells, span_cells)
    target_plane = inflow_plane + jnp.array([1.0, 0.0, 0.0, 0.0, 0.0], jnp.float32)[:, None, None]
    wind_first = stream_pos * wind_cells
    relax_rate = relax_weights(
        wind_first + jnp.arange(wind_cells, dtype=jnp.int32), wind_cells // 2
    )

    def advance(state):
        padded = extended(state, (("stream", 3), ("span", 2), ("vert", 1)), 1)
        return rates(padded, solid_frac, relax_rate, target_plane)

    first_update = fields + time_step * advance(fields)
    second_rate = advance(first_update)
    new_fields = 0.5 * (fields + first_update + time_step * second_rate)
    pressure = new_fields[3].reshape(-1)
    sampled = pressure[deck_cells[0, 0, 0]]
    strip_count = mode_shapes.shape[1]
    rows_all = lax.all_gather(sampled.reshape(1, 1, 1, -1), "span", axis=1, tiled=True)
    traction = rows_all[0, :, 0][:, None, :] * deck_geom[0, :, 0]
    forces = strip_forces(traction, strip_ids[0, :, 0], strip_count)
    modal_part = jnp.einsum("cj,cjm->m", forces, mode_shapes, precision=lax.Precision.HIGHEST)
    modal_force = lax.psum(modal_part, ("stream", "vert"))
    return (new_fields, modal_force)


def solution(mesh):
    return jax.shard_map(
        on_device,
        mesh=mesh,
        in_specs=(
            P(None, "vert", "span", "stream"),
            P("vert", "span", "stream"),
            P(("stream", "span", "vert"), None, None),
            P(("stream", "span", "vert"), None),
            P("vert", "span", "stream", None),
            P("vert", None, "stream", None, None),
            P("vert", None, "stream", None),
            P(),
        ),
        out_specs=(P(None, "vert", "span", "stream"), P()),
        check_vma=False,
    )
```

profile of v0, /device:TPU:0, one launch (start us, length us, event | category | flops | bytes accessed | tf_op | source)
XLA Modules:
  0.0 156.2 jit_solution(6153192793725801816)
XLA Ops:
  0.6 2.2 %fusion.52 = (f32[5,32,16,1]{3,2,1,0:T(8,128)S(1)}, f32[5,32,16,1]{3,2,1,0:T(8,128)S(1)}) fusion(f32[5,32,16,128]{3,2,1,0:T(8,128)} %param.13), kind=kLoop, calls=%fused_computation.163 | loop fusion | bytes 40960 | tf_op jit(solution)/shard_map/slice | solution.py:28
  3.5 1.4 collective-permute-start
  5.5 4.9 %collective-permute-start.1 = (f32[5,32,16,1]{1,2,3,0:T(8,128)S(1)}, f32[5,32,16,1]{1,2,3,0:T(8,128)S(1)}, u32[]{:S(2)}, u32[]{:S(2)}) collective-permute-start(f32[5,32,16,1]{1,2,3,0:T(8,128)S(1)} %copy.56), channel_id=1, source_target_pairs={{0,16},{1,17},{2,18},{3,19},{4,20},{5,21},{6,22},{7,23},{8,24},{9,... | collective-permute-start | bytes 30728 | tf_op jit(solution)/shard_map/ppermute | solution.py:27
  11.0 0.8 all_to_all.8
  11.8 7.1 %all-to-all-start = ((f32[16,1,2560]{2,1,0:T(1,128)}), f32[16,1,2560]{2,1,0:T(1,128)}, u32[]{:S(2)}, u32[]{:S(2)}) async-start(f32[16,1,2560]{2,1,0:T(1,128)} %all_to_all.8), calls=%async_computation | async-start | bytes 327680 | tf_op jit(solution)/shard_map/all_to_all | solution.py:131
  18.9 0.9 bitcast_multiply_fusion.5
  20.0 1.8 %fusion.45 = (f32[128,512]{0,1:T(8,128)S(1)}, f32[128,512]{0,1:T(8,128)}) fusion(s32[128,32,16]{0,2,1:T(8,128)S(1)} %broadcast_add_fusion), kind=kLoop, calls=%fused_computation.138 | loop fusion | flops 851968 | bytes 786432 | tf_op jit(solution)/shard_map/cos | solution.py:44
  21.8 0.6 copy.37
  22.5 1.6 %copy.39 = f32[5,32,16,1]{3,2,1,0:T(8,128)} copy(f32[5,32,16,1]{1,2,3,0:T(8,128)S(1)} %collective-permute-done.1) | data formatting | bytes 20480 | tf_op jit(solution)/shard_map/ppermute | solution.py:27
  24.1 2.5 %pad_maximum_fusion.39 = (f32[5,32,1,130]{3,2,1,0:T(1,128)S(1)}, f32[5,32,1,130]{3,2,1,0:T(1,128)S(1)}) fusion(f32[5,32,16,1]{3,2,1,0:T(8,128)S(1)} %copy.37, f32[5,32,16,128]{3,2,1,0:T(8,128)S(1)} %copy-done.1, f32[5,32,16,1]{3,2,1,0:T(8,128)} %copy.39), kind=kLoop, calls=%fused_computation.120 | loop fusion | flops 83200 | bytes 1497600 | tf_op jit(solution)/shard_map/concatenate | solution.py:31
  26.6 1.3 collective-permute-start.2
  27.9 4.6 %collective-permute-start.3 = (f32[5,32,1,130]{3,2,1,0:T(1,128)S(1)}, f32[5,32,1,130]{3,2,1,0:T(1,128)S(1)}, u32[]{:S(2)}, u32[]{:S(2)}) collective-permute-start(f32[5,32,1,130]{3,2,1,0:T(1,128)S(1)} %get-tuple-element.79), channel_id=1, source_target_pairs={{0,4},{4,8},{8,12},{1,5},{5,9},{9,13},{2,6},{6,10},{10,14},{3,7},{... | collective-permute-start | bytes 249608 | tf_op jit(solution)/shard_map/ppermute | solution.py:27
  32.5 2.5 %collective-permute-done.2 = f32[5,32,1,130]{3,2,1,0:T(1,128)S(1)} collective-permute-done((f32[5,32,1,130]{3,2,1,0:T(1,128)S(1)}, f32[5,32,1,130]{3,2,1,0:T(1,128)S(1)}, u32[]{:S(2)}, u32[]{:S(2)}) %collective-permute-start.2) | collective-permute-done | bytes 83232 | tf_op jit(solution)/shard_map/ppermute | solution.py:30
  35.0 1.2 collective-permute-done.3
  36.3 1.3 collective-permute-start.4
  37.6 3.0 %collective-permute-start.5 = (f32[5,1,18,130]{3,2,1,0:T(8,128)S(1)}, f32[5,1,18,130]{3,2,1,0:T(8,128)S(1)}, u32[]{:S(2)}, u32[]{:S(2)}) collective-permute-start(f32[5,1,18,130]{3,2,1,0:T(8,128)S(1)} %get-tuple-element.71), channel_id=1, source_target_pairs={{0,1},{1,2},{2,3},{4,5},{5,6},{6,7},{8,9},{9,10},{10,11},{12,13},{... | collective-permute-start | bytes 140408 | tf_op jit(solution)/shard_map/ppermute | solution.py:27
  40.7 1.1 broadcast_multiply_fusion.4
  41.9 3.2 %broadcast_multiply_fusion.3 = (f32[5,32,16,128]{3,2,1,0:T(8,128)S(1)}, f32[5,32,16,128]{3,2,1,0:T(8,128)S(1)}) fusion(f32[5,1,18,130]{3,2,1,0:T(8,128)S(1)} %collective-permute-done.4, f32[5,32,1,130]{3,2,1,0:T(1,128)S(1)} %collective-permute-done.2, f32[5,32,16,1]{3,2,1,0:T(8,128)S(1)} %copy.37, f32[5,32,16,128]{3,2,1,0:T(8,128)S(1)} %copy-done.1, ...), kind=kLoop, calls=%fused_computation.50 | loop fusion | flops 5242880 | bytes 4212640 | tf_op jit(solution)/shard_map/mul | solution.py:62
  45.1 0.8 fusion.40
  45.9 0.8 fusion.36
  46.6 0.8 fusion.32
  47.4 0.8 fusion.27
  48.2 0.7 broadcast_dynamic-update-slice_fusion.1
  48.9 1.3 reduce
  50.9 7.7 %psum.14 = f32[5,32,16]{2,1,0:T(8,128)S(1)} all-reduce(f32[5,32,16]{2,1,0:T(8,128)S(1)} %reshape.200), channel_id=1, replica_groups=mesh['stream'=2,'span'=4,'vert'=4] {'stream'}, use_global_device_ids=true, to_apply=%region_3.4 | all-reduce | flops 2560 | bytes 20480 | tf_op jit(solution)/shard_map/psum | solution.py:147
  58.8 7.8 %multiply_add_fusion = f32[5,32,16,128]{3,2,1,0:T(8,128)S(1)} fusion(f32[5,32,16,128]{3,2,1,0:T(8,128)S(1)} %copy-done.1, f32[5,32,16,128]{3,2,1,0:T(8,128)} %broadcast_dynamic-update-slice_fusion.1, f32[5,32,16]{2,1,0:T(8,128)S(1)} %broadcast_add_fusion.1, f32[128]{0:T(128)S(1)} %compare_select_fusion.1, f32[32,16,128]{2,1,0:T(8,128)} %get-tuple-element.87, ...), kind=kLoop, calls=%fused_computation.45 | loop fusion | flops 13434880 | bytes 5009844 | tf_op jit(solution)/shard_map/add | solution.py:158
  66.6 1.9 %fusion.51 = (f32[5,32,16,1]{3,2,1,0:T(8,128)}, f32[5,32,16,1]{3,2,1,0:T(8,128)}) fusion(f32[5,32,16,128]{3,2,1,0:T(8,128)S(1)} %multiply_add_fusion), kind=kLoop, calls=%fused_computation.162 | loop fusion | bytes 40960 | tf_op jit(solution)/shard_map/slice | solution.py:28
  68.5 1.9 %copy.44 = f32[5,32,16,1]{1,2,3,0:T(8,128)S(1)} copy(f32[5,32,16,1]{3,2,1,0:T(8,128)} %get-tuple-element.85) | data formatting | bytes 20480 | tf_op jit(solution)/shard_map/slice | solution.py:30
  70.4 1.3 collective-permute-start.6
  71.7 1.9 %copy.46 = f32[5,32,16,1]{1,2,3,0:T(8,128)S(1)} copy(f32[5,32,16,1]{3,2,1,0:T(8,128)} %get-tuple-element.84) | data formatting | bytes 20480 | tf_op jit(solution)/shard_map/slice | solution.py:28
  73.6 4.5 %collective-permute-start.7 = (f32[5,32,16,1]{1,2,3,0:T(8,128)S(1)}, f32[5,32,16,1]{1,2,3,0:T(8,128)S(1)}, u32[]{:S(2)}, u32[]{:S(2)}) collective-permute-start(f32[5,32,16,1]{1,2,3,0:T(8,128)S(1)} %copy.46), channel_id=1, source_target_pairs={{0,16},{1,17},{2,18},{3,19},{4,20},{5,21},{6,22},{7,23},{8,24},{9,... | collective-permute-start | bytes 30728 | tf_op jit(solution)/shard_map/ppermute | solution.py:27
  78.2 1.6 %copy.45 = f32[5,32,16,1]{3,2,1,0:T(8,128)} copy(f32[5,32,16,1]{1,2,3,0:T(8,128)S(1)} %collective-permute-done.6) | data formatting | bytes 20480 | tf_op jit(solution)/shard_map/ppermute | solution.py:30
  79.8 1.6 %copy.47 = f32[5,32,16,1]{3,2,1,0:T(8,128)} copy(f32[5,32,16,1]{1,2,3,0:T(8,128)S(1)} %collective-permute-done.7) | data formatting | bytes 20480 | tf_op jit(solution)/shard_map/ppermute | solution.py:27
  81.5 2.9 %pad_maximum_fusion.36 = (f32[5,32,1,130]{3,2,1,0:T(1,128)S(1)}, f32[5,32,1,130]{3,2,1,0:T(1,128)S(1)}) fusion(f32[5,32,16,1]{3,2,1,0:T(8,128)} %copy.45, f32[5,32,16,128]{3,2,1,0:T(8,128)S(1)} %multiply_add_fusion, f32[5,32,16,1]{3,2,1,0:T(8,128)} %copy.47), kind=kLoop, calls=%fused_computation.117 | loop fusion | flops 83200 | bytes 1497600 | tf_op jit(solution)/shard_map/concatenate | solution.py:31
  84.4 1.4 collective-permute-start.8
  85.8 5.0 %collective-permute-start.9 = (f32[5,32,1,130]{3,2,1,0:T(1,128)S(1)}, f32[5,32,1,130]{3,2,1,0:T(1,128)S(1)}, u32[]{:S(2)}, u32[]{:S(2)}) collective-permute-start(f32[5,32,1,130]{3,2,1,0:T(1,128)S(1)} %get-tuple-element.75), channel_id=1, source_target_pairs={{0,4},{4,8},{8,12},{1,5},{5,9},{9,13},{2,6},{6,10},{10,14},{3,7},{... | collective-permute-start | bytes 249608 | tf_op jit(solution)/shard_map/ppermute | solution.py:27
  90.9 1.9 %collective-permute-done.8 = f32[5,32,1,130]{3,2,1,0:T(1,128)S(1)} collective-permute-done((f32[5,32,1,130]{3,2,1,0:T(1,128)S(1)}, f32[5,32,1,130]{3,2,1,0:T(1,128)S(1)}, u32[]{:S(2)}, u32[]{:S(2)}) %collective-permute-start.8) | collective-permute-done | bytes 83232 | tf_op jit(solution)/shard_map/ppermute | solution.py:30
  92.9 1.2 collective-permute-done.9
  94.2 1.3 collective-permute-start.10
  95.5 3.0 %collective-permute-start.11 = (f32[5,1,18,130]{3,2,1,0:T(8,128)S(1)}, f32[5,1,18,130]{3,2,1,0:T(8,128)S(1)}, u32[]{:S(2)}, u32[]{:S(2)}) collective-permute-start(f32[5,1,18,130]{3,2,1,0:T(8,128)S(1)} %get-tuple-element.69), channel_id=1, source_target_pairs={{0,1},{1,2},{2,3},{4,5},{5,6},{6,7},{8,9},{9,10},{10,11},{12,13},{... | collective-permute-start | bytes 140408 | tf_op jit(solution)/shard_map/ppermute | solution.py:27
  98.6 1.1 broadcast_multiply_fusion.1
  99.7 3.2 %broadcast_multiply_fusion = (f32[5,32,16,128]{3,2,1,0:T(8,128)S(1)}, f32[5,32,16,128]{3,2,1,0:T(8,128)S(1)}) fusion(f32[5,1,18,130]{3,2,1,0:T(8,128)S(1)} %collective-permute-done.10, f32[5,32,1,130]{3,2,1,0:T(1,128)S(1)} %collective-permute-done.8, f32[5,32,16,1]{3,2,1,0:T(8,128)S(1)} %copy-done.4, f32[5,32,16,128]{3,2,1,0:T(8,128)S(1)} %multiply_add_fusion, ...), kind=kLoop, calls=%fused_computation.47 | loop fusion | flops 5242880 | bytes 4212640 | tf_op jit(solution)/shard_map/mul | solution.py:62
  103.2 5.0 %add_multiply_fusion = f32[5,32,16,128]{3,2,1,0:T(8,128)S(1)} fusion(f32[5,32,16,128]{3,2,1,0:T(8,128)S(1)} %broadcast_dynamic-update-slice_fusion, f32[5,32,16,128]{3,2,1,0:T(8,128)S(1)} %multiply_add_fusion, f32[5,32,16,128]{3,2,1,0:T(8,128)S(1)} %copy-done.1, f32[32,16,128]{2,1,0:T(8,128)S(1)} %get-tuple-element.82, ...), kind=kLoop, calls=%fused_computation.44 | loop fusion | flops 14090240 | bytes 6320564 | tf_op jit(solution)/shard_map/mul | solution.py:160
  108.2 1.0 copy-done.7
  109.3 11.8 %gather_fusion = f32[2048]{0:T(1024)S(1)} fusion(f32[65536]{0:T(1024)S(1)} %bitcast.150, s32[2048]{0:T(1024)S(1)} %broadcast_clamp_fusion), kind=kCustom, calls=%fused_computation | custom fusion | bytes 24576 | tf_op jit(solution)/shard_map/gather | solution.py:162
  121.1 14.5 %all-gather = f32[8192]{0:T(1024)S(1)} all-gather(f32[2048]{0:T(1024)S(1)} %gather_fusion), channel_id=2, replica_groups=mesh['stream'=2,'span'=4,'vert'=4] {'span'}, dimensions={0}, use_global_device_ids=true | all-gather | bytes 40960 | tf_op jit(solution)/shard_map/all_gather | solution.py:164
  135.7 2.6 %while.11 = (s32[]{:T(128)}, f32[3,16]{1,0:T(4,128)S(1)}, f32[4,3,2048]{2,0,1:T(4,128)S(1)}, s32[4,2048]{1,0:T(4,128)S(1)}, s32[]{:T(128)}, /*index=5*/s32[]{:T(128)}) while((s32[]{:T(128)}, f32[3,16]{1,0:T(4,128)S(1)}, f32[4,3,2048]{2,0,1:T(4,128)S(1)}, s32[4,2048]{1,0:T(4,128)S(1)}, s32[]{:T(128)}, /*index=5*/s32[]{:T(128)}) %tuple.46), condition=%wide.region_5.6_spmd.clone, body=%wide.region_4.5_spmd.clone.sunk | while | flops 1212515 | bytes 98775 | solution.py:107
  138.5 17.7 %psum.15 = f32[32]{0:T(128)} all-reduce(f32[32]{0:T(128)S(1)} %convolution_bitcast_fusion), channel_id=1, replica_groups=mesh['stream'=2,'span'=4,'vert'=4] {'stream','vert'}, use_global_device_ids=true, to_apply=%region_6.7 | all-reduce | flops 32 | bytes 256 | tf_op jit(solution)/shard_map/psum | solution.py:168
  (94 shorter events, 6.2 us)
Async XLA Ops:
  0.6 137.7 %copy-start = (f32[3,16,32]{2,1,0:T(8,128)S(1)}, f32[3,16,32]{2,1,0:T(8,128)}, u32[]{:S(2)}) copy-start(f32[3,16,32]{2,1,0:T(8,128)} %param.20) | copy-start | bytes 18436
  2.9 7.6 %copy-start.16 = (s32[16,1]{0,1:T(1,128)S(1)}, s32[16,1]{0,1:T(1,128)}, u32[]{:S(2)}) copy-start(s32[16,1]{0,1:T(1,128)} %param.16) | copy-start | bytes 196
  2.9 7.8 %copy-start.12 = (f32[16,5,256]{2,0,1:T(8,128)S(1)}, f32[16,5,256]{2,0,1:T(8,128)}, u32[]{:S(2)}) copy-start(f32[16,5,256]{2,0,1:T(8,128)} %param.15) | copy-start | bytes 245764
  3.5 15.4 %copy-start.1 = (f32[5,32,16,128]{3,2,1,0:T(8,128)S(1)}, f32[5,32,16,128]{3,2,1,0:T(8,128)}, u32[]{:S(2)}) copy-start(f32[5,32,16,128]{3,2,1,0:T(8,128)} %param.13) | copy-start | bytes 3932164
  3.5 18.3 %collective-permute-start = (f32[5,32,16,1]{1,2,3,0:T(8,128)S(1)}, f32[5,32,16,1]{1,2,3,0:T(8,128)S(1)}, u32[]{:S(2)}, u32[]{:S(2)}) collective-permute-start(f32[5,32,16,1]{1,2,3,0:T(8,128)S(1)} %copy.55), channel_id=1, source_target_pairs={{16,0},{17,1},{18,2},{19,3},{20,4},{21,5},{22,6},{23,7},{24,8},{25... | collective-permute-start | bytes 30728 | tf_op jit(solution)/shard_map/ppermute | solution.py:30
  5.5 16.9 %collective-permute-start.1 = (f32[5,32,16,1]{1,2,3,0:T(8,128)S(1)}, f32[5,32,16,1]{1,2,3,0:T(8,128)S(1)}, u32[]{:S(2)}, u32[]{:S(2)}) collective-permute-start(f32[5,32,16,1]{1,2,3,0:T(8,128)S(1)} %copy.56), channel_id=1, source_target_pairs={{0,16},{1,17},{2,18},{3,19},{4,20},{5,21},{6,22},{7,23},{8,24},{9,... | collective-permute-start | bytes 30728 | tf_op jit(solution)/shard_map/ppermute | solution.py:27
  10.7 9.1 %copy-start.14 = (s32[1,1,1,2048]{3,2,1,0:T(1,128)S(1)}, s32[1,1,1,2048]{3,2,1,0:T(1,128)}, u32[]{:S(2)}) copy-start(s32[1,1,1,2048]{3,2,1,0:T(1,128)} %param.17) | copy-start | bytes 24580
  11.8 37.1 %all-to-all-start = ((f32[16,1,2560]{2,1,0:T(1,128)}), f32[16,1,2560]{2,1,0:T(1,128)}, u32[]{:S(2)}, u32[]{:S(2)}) async-start(f32[16,1,2560]{2,1,0:T(1,128)} %all_to_all.8), calls=%async_computation | async-start | bytes 327680 | tf_op jit(solution)/shard_map/all_to_all | solution.py:131
  22.5 19.4 %copy-start.2 = (f32[5,32,16,1]{3,2,1,0:T(8,128)}, f32[5,32,16,1]{3,2,1,0:T(8,128)S(1)}, u32[]{:S(2)}) copy-start(f32[5,32,16,1]{3,2,1,0:T(8,128)S(1)} %copy.37) | copy-start | bytes 30724
  24.1 12.1 %copy-start.3 = (f32[5,32,16,1]{3,2,1,0:T(8,128)S(1)}, f32[5,32,16,1]{3,2,1,0:T(8,128)}, u32[]{:S(2)}) copy-start(f32[5,32,16,1]{3,2,1,0:T(8,128)} %copy.39) | copy-start | bytes 30724
  26.6 8.4 %collective-permute-start.2 = (f32[5,32,1,130]{3,2,1,0:T(1,128)S(1)}, f32[5,32,1,130]{3,2,1,0:T(1,128)S(1)}, u32[]{:S(2)}, u32[]{:S(2)}) collective-permute-start(f32[5,32,1,130]{3,2,1,0:T(1,128)S(1)} %get-tuple-element.80), channel_id=1, source_target_pairs={{4,0},{8,4},{12,8},{5,1},{9,5},{13,9},{6,2},{10,6},{14,10},{7,3},{... | collective-permute-start | bytes 249608 | tf_op jit(solution)/shard_map/ppermute | solution.py:30
  27.9 8.2 %collective-permute-start.3 = (f32[5,32,1,130]{3,2,1,0:T(1,128)S(1)}, f32[5,32,1,130]{3,2,1,0:T(1,128)S(1)}, u32[]{:S(2)}, u32[]{:S(2)}) collective-permute-start(f32[5,32,1,130]{3,2,1,0:T(1,128)S(1)} %get-tuple-element.79), channel_id=1, source_target_pairs={{0,4},{4,8},{8,12},{1,5},{5,9},{9,13},{2,6},{6,10},{10,14},{3,7},{... | collective-permute-start | bytes 249608 | tf_op jit(solution)/shard_map/ppermute | solution.py:27
  36.3 5.5 %collective-permute-start.4 = (f32[5,1,18,130]{3,2,1,0:T(8,128)S(1)}, f32[5,1,18,130]{3,2,1,0:T(8,128)S(1)}, u32[]{:S(2)}, u32[]{:S(2)}) collective-permute-start(f32[5,1,18,130]{3,2,1,0:T(8,128)S(1)} %get-tuple-element.72), channel_id=1, source_target_pairs={{1,0},{2,1},{3,2},{5,4},{6,5},{7,6},{9,8},{10,9},{11,10},{13,12},{... | collective-permute-start | bytes 140408 | tf_op jit(solution)/shard_map/ppermute | solution.py:30
  37.6 4.2 %collective-permute-start.5 = (f32[5,1,18,130]{3,2,1,0:T(8,128)S(1)}, f32[5,1,18,130]{3,2,1,0:T(8,128)S(1)}, u32[]{:S(2)}, u32[]{:S(2)}) collective-permute-start(f32[5,1,18,130]{3,2,1,0:T(8,128)S(1)} %get-tuple-element.71), channel_id=1, source_target_pairs={{0,1},{1,2},{2,3},{4,5},{5,6},{6,7},{8,9},{9,10},{10,11},{12,13},{... | collective-permute-start | bytes 140408 | tf_op jit(solution)/shard_map/ppermute | solution.py:27
  41.8 3.3 %copy-start.6 = (f32[32,16,128]{2,1,0:T(8,128)S(1)}, f32[32,16,128]{2,1,0:T(8,128)}, u32[]{:S(2)}) copy-start(f32[32,16,128]{2,1,0:T(8,128)} %param.14) | copy-start | bytes 786436
  41.8 3.2 %copy-start.9 = (f32[5,1,18,130]{3,2,1,0:T(8,128)}, f32[5,1,18,130]{3,2,1,0:T(8,128)S(1)}, u32[]{:S(2)}) copy-start(f32[5,1,18,130]{3,2,1,0:T(8,128)S(1)} %collective-permute-done.4) | copy-start | bytes 140404
  41.9 3.2 %copy-start.10 = (f32[5,1,18,130]{3,2,1,0:T(8,128)}, f32[5,1,18,130]{3,2,1,0:T(8,128)S(1)}, u32[]{:S(2)}) copy-start(f32[5,1,18,130]{3,2,1,0:T(8,128)S(1)} %collective-permute-done.5) | copy-start | bytes 140404
  47.4 2.9 %copy-start.8 = (f32[128,512]{0,1:T(8,128)S(1)}, f32[128,512]{0,1:T(8,128)}, u32[]{:S(2)}) copy-start(f32[128,512]{0,1:T(8,128)} %get-tuple-element.92) | copy-start | bytes 786436
  47.4 11.3 %copy-start.17 = (f32[5]{0:T(128)S(1)}, f32[5]{0:T(128)}, u32[]{:S(2)}) copy-start(f32[5]{0:T(128)} %constant.113.clone) | copy-start | bytes 64
  47.4 11.4 %copy-start.15 = (f32[5]{0:T(128)S(1)}, f32[5]{0:T(128)}, u32[]{:S(2)}) copy-start(f32[5]{0:T(128)} %constant.114.clone) | copy-start | bytes 64
  68.5 9.6 %copy-start.13 = (s32[1,4,1,2048]{3,2,1,0:T(1,128)S(1)}, s32[1,4,1,2048]{3,2,1,0:T(1,128)}, u32[]{:S(2)}) copy-start(s32[1,4,1,2048]{3,2,1,0:T(1,128)} %param.19) | copy-start | bytes 98308
  70.4 7.8 %collective-permute-start.6 = (f32[5,32,16,1]{1,2,3,0:T(8,128)S(1)}, f32[5,32,16,1]{1,2,3,0:T(8,128)S(1)}, u32[]{:S(2)}, u32[]{:S(2)}) collective-permute-start(f32[5,32,16,1]{1,2,3,0:T(8,128)S(1)} %copy.44), channel_id=1, source_target_pairs={{16,0},{17,1},{18,2},{19,3},{20,4},{21,5},{22,6},{23,7},{24,8},{25... | collective-permute-start | bytes 30728 | tf_op jit(solution)/shard_map/ppermute | solution.py:30
  73.6 6.2 %collective-permute-start.7 = (f32[5,32,16,1]{1,2,3,0:T(8,128)S(1)}, f32[5,32,16,1]{1,2,3,0:T(8,128)S(1)}, u32[]{:S(2)}, u32[]{:S(2)}) collective-permute-start(f32[5,32,16,1]{1,2,3,0:T(8,128)S(1)} %copy.46), channel_id=1, source_target_pairs={{0,16},{1,17},{2,18},{3,19},{4,20},{5,21},{6,22},{7,23},{8,24},{9,... | collective-permute-start | bytes 30728 | tf_op jit(solution)/shard_map/ppermute | solution.py:27
  81.5 12.6 %copy-start.5 = (f32[5,32,16,1]{3,2,1,0:T(8,128)S(1)}, f32[5,32,16,1]{3,2,1,0:T(8,128)}, u32[]{:S(2)}) copy-start(f32[5,32,16,1]{3,2,1,0:T(8,128)} %copy.47) | copy-start | bytes 30724
  84.4 9.7 %copy-start.4 = (f32[5,32,16,1]{3,2,1,0:T(8,128)S(1)}, f32[5,32,16,1]{3,2,1,0:T(8,128)}, u32[]{:S(2)}) copy-start(f32[5,32,16,1]{3,2,1,0:T(8,128)} %copy.45) | copy-start | bytes 30724
  84.4 8.5 %collective-permute-start.8 = (f32[5,32,1,130]{3,2,1,0:T(1,128)S(1)}, f32[5,32,1,130]{3,2,1,0:T(1,128)S(1)}, u32[]{:S(2)}, u32[]{:S(2)}) collective-permute-start(f32[5,32,1,130]{3,2,1,0:T(1,128)S(1)} %get-tuple-element.76), channel_id=1, source_target_pairs={{4,0},{8,4},{12,8},{5,1},{9,5},{13,9},{6,2},{10,6},{14,10},{7,3},{... | collective-permute-start | bytes 249608 | tf_op jit(solution)/shard_map/ppermute | solution.py:30
  85.8 8.2 %collective-permute-start.9 = (f32[5,32,1,130]{3,2,1,0:T(1,128)S(1)}, f32[5,32,1,130]{3,2,1,0:T(1,128)S(1)}, u32[]{:S(2)}, u32[]{:S(2)}) collective-permute-start(f32[5,32,1,130]{3,2,1,0:T(1,128)S(1)} %get-tuple-element.75), channel_id=1, source_target_pairs={{0,4},{4,8},{8,12},{1,5},{5,9},{9,13},{2,6},{6,10},{10,14},{3,7},{... | collective-permute-start | bytes 249608 | tf_op jit(solution)/shard_map/ppermute | solution.py:27
  94.2 5.5 %collective-permute-start.10 = (f32[5,1,18,130]{3,2,1,0:T(8,128)S(1)}, f32[5,1,18,130]{3,2,1,0:T(8,128)S(1)}, u32[]{:S(2)}, u32[]{:S(2)}) collective-permute-start(f32[5,1,18,130]{3,2,1,0:T(8,128)S(1)} %get-tuple-element.70), channel_id=1, source_target_pairs={{1,0},{2,1},{3,2},{5,4},{6,5},{7,6},{9,8},{10,9},{11,10},{13,12},{... | collective-permute-start | bytes 140408 | tf_op jit(solution)/shard_map/ppermute | solution.py:30
  95.5 4.2 %collective-permute-start.11 = (f32[5,1,18,130]{3,2,1,0:T(8,128)S(1)}, f32[5,1,18,130]{3,2,1,0:T(8,128)S(1)}, u32[]{:S(2)}, u32[]{:S(2)}) collective-permute-start(f32[5,1,18,130]{3,2,1,0:T(8,128)S(1)} %get-tuple-element.69), channel_id=1, source_target_pairs={{0,1},{1,2},{2,3},{4,5},{5,6},{6,7},{8,9},{9,10},{10,11},{12,13},{... | collective-permute-start | bytes 140408 | tf_op jit(solution)/shard_map/ppermute | solution.py:27
  108.2 1.1 copy-start.7
  109.3 26.3 %copy-start.11 = (f32[1,4,1,3,2048]{4,2,3,1,0:T(1,128)S(1)}, f32[1,4,1,3,2048]{4,2,3,1,0:T(1,128)}, u32[]{:S(2)}) copy-start(f32[1,4,1,3,2048]{4,2,3,1,0:T(1,128)} %param.18) | copy-start | bytes 294916
where the time goes:
time: 157 us; the launch traced here: 156 us
  starting transfers between devices  40.1 us (26%)
  blocking collectives  39.9 us (25%)
  other arithmetic  35.2 us (22%)
  local copies, waits for them, and re-layouts  29.5 us (19%)
  waiting for transfers between devices  6.79 us (4%)
  matrix products  3.25 us (2%)
    ppermute x6, starting transfers between devices, extended(): lax.ppermute(lax.slice_in_dim(block, block.shape[dim] - width, None, axis...  25.1 us
    psum x1, blocking collectives, on_device(): modal_force = lax.psum(modal_part, ('stream', 'vert'))  17.7 us
    all_gather x1, blocking collectives, on_device(): lax.all_gather(sampled.reshape(1, 1, 1, -1), 'span', axis=1, tiled=True)  14.5 us
    gather x1, local copies, waits for them, and re-layouts, on_device(): sampled = pressure[deck_cells[0, 0, 0]]  11.8 us
    ppermute x6, starting transfers between devices, extended(): lax.ppermute(lax.slice_in_dim(block, 0, width, axis=dim), axis, backward)  8 us
    add x1, other arithmetic, on_device(): first_update = fields + time_step * advance(fields)  7.84 us
    psum x1, blocking collectives, on_device(): lax.psum(partial_value, 'stream').reshape(5, depth_cells, span_cells)  7.73 us
    all_to_all x1, starting transfers between devices, on_device(): lax.all_to_all(outgoing.reshape(tile_count, CAP * 5 * spec_cols), ('span'...  7.07 us
  transfers between devices with their start and end apart: 13, of which 4 were waited for; matrix products, arithmetic and copies ran while one was open for 14% of the time, Pallas kernels for 0%

commit v1 on v0

v1 whole, which is shorter than its diff:
```python
import functools
import math

import jax
import jax.numpy as jnp
from jax import lax
from jax.experimental import pallas as pl
from jax.experimental.pallas import tpu as pltpu
from jax.sharding import PartitionSpec as P

MESH = pl.DeviceIdType.MESH
HIGHEST = lax.Precision.HIGHEST

time_step = 0.15
viscous = 0.05
heat_diff = 0.03
sound_sq = 1.0
buoyant = 0.5
penalty = 0.5
relax_time = 0.5
relax_depth = 8.0
wave_cols = 16
FIELDS = 5
ROWS = 8
PARTS = 2


def split_index(values, size):
    if size & (size - 1) == 0:
        return values >> (size.bit_length() - 1), values & (size - 1)
    whole = lax.div(values, jnp.int32(size))
    return whole, values - whole * size


def circle(turns):
    quarter = jnp.floor(4.0 * turns + 0.5)
    angle = (turns - 0.25 * quarter) * (2.0 * math.pi)
    sq = angle * angle
    sine = angle * (
        1.0 + sq * (-1.0 / 6 + sq * (1.0 / 120 + sq * (-1.0 / 5040 + sq * (1.0 / 362880))))
    )
    cosine = 1.0 + sq * (
        -0.5 + sq * (1.0 / 24 + sq * (-1.0 / 720 + sq * (1.0 / 40320 + sq * (-1.0 / 3628800))))
    )
    odd = (quarter == 1.0) | (quarter == 3.0)
    cos_flip = jnp.where((quarter == 1.0) | (quarter == 2.0), -1.0, 1.0)
    sin_flip = jnp.where((quarter == 2.0) | (quarter == 3.0), -1.0, 1.0)
    return cos_flip * jnp.where(odd, sine, cosine), sin_flip * jnp.where(odd, cosine, sine)


def kernel(
    sizes,
    fields_ref,
    solid_ref,
    panels_ref,
    owner_ref,
    cells_ref,
    geom_ref,
    strips_ref,
    modes_ref,
    out_ref,
    modal_ref,
    state,
    update,
    result,
    x_send,
    x_recv,
    x_both,
    y_send,
    y_recv,
    pan_in,
    pan_send,
    pan_recv,
    co_send,
    co_recv,
    wave,
    target,
    press,
    md_send,
    md_recv,
    sd_send,
    sd_recv,
    local_sem,
    halo_s,
    halo_r,
    pan_s,
    pan_r,
    co_s,
    co_r,
    md_s,
    md_r,
    sd_s,
    sd_r,
):
    n_stream, n_span, n_vert = sizes
    tiles = n_span * n_vert
    depth, span_cells, wind = fields_ref.shape[1:]
    half = depth // PARTS
    per_group = min(FIELDS, (wind // 2) // half)
    groups = -(-FIELDS // per_group)
    held = panels_ref.shape[0]
    spec_cols = panels_ref.shape[2]
    spec = spec_cols // 2
    strip_share = modes_ref.shape[1] // n_span
    n_modes = modes_ref.shape[2]
    deck = cells_ref.shape[3]
    me = (lax.axis_index("stream"), lax.axis_index("span"), lax.axis_index("vert"))
    stream_pos, span_pos, vert_pos = me
    my_tile = span_pos * n_vert + vert_pos

    def tile_peer(step):
        peer = lax.rem(my_tile + step, tiles)
        whole = lax.div(peer, jnp.int32(n_vert))
        return peer, (stream_pos, whole, peer - whole * n_vert)

    def stream_peer(step):
        peer = lax.rem(stream_pos + step, n_stream)
        return peer, (peer, span_pos, vert_pos)

    load = pltpu.make_async_copy(fields_ref, state.at[:, pl.ds(1, depth)], local_sem.at[0])
    load.start()

    barrier = pltpu.get_barrier_semaphore()
    for step in range(1, tiles):
        pl.semaphore_signal(barrier, inc=1, device_id=tile_peer(step)[1], device_id_type=MESH)
    for step in range(1, n_stream):
        pl.semaphore_signal(barrier, inc=1, device_id=stream_peer(step)[1], device_id_type=MESH)

    pan_in[...] = jnp.zeros_like(pan_in)
    pan_in[:, 0:FIELDS, :] = panels_ref[...]
    owner = jnp.broadcast_to(owner_ref[...], (held, tiles * ROWS))
    owner = jnp.broadcast_to(owner[:, None, :], (held, ROWS, tiles * ROWS))
    owner = owner.reshape(held * ROWS, tiles * ROWS)
    row_field = lax.broadcasted_iota(jnp.int32, owner.shape, 0) & (ROWS - 1)
    col_tile, col_field = split_index(lax.broadcasted_iota(jnp.int32, owner.shape, 1), ROWS)
    route = jnp.where((owner == col_tile) & (row_field == col_field), 1.0, 0.0)
    sums = lax.dot_general(
        route,
        pan_in[...].reshape(held * ROWS, spec_cols),
        (((0,), (0,)), ((), ())),
        precision=HIGHEST,
        preferred_element_type=jnp.float32,
    )
    pan_send[...] = sums.reshape(tiles, ROWS, spec_cols)

    def halo(axis, way, src, dst, sem):
        count, place = sizes[axis], me[axis]
        up = way == 0
        to = lax.rem(place + (1 if up else count - 1), count)
        device = tuple(to if a == axis else me[a] for a in range(3))
        sends = place < count - 1 if up else place > 0
        gets = place > 0 if up else place < count - 1

        def copy():
            return pltpu.make_async_remote_copy(
                src_ref=src,
                dst_ref=dst,
                send_sem=halo_s.at[sem],
                recv_sem=halo_r.at[sem],
                device_id=device,
                device_id_type=MESH,
            )

        def start():
            pl.when(sends)(lambda: copy().start())

        def arrive():
            pl.when(gets)(lambda: copy().wait_recv())

        def leave():
            pl.when(sends)(lambda: copy().wait_send())

        def clear():
            @pl.when(jnp.logical_not(gets))
            def _():
                dst[...] = jnp.zeros(dst.shape, jnp.float32)

        return start, arrive, leave, clear

    z_first = [
        halo(2, 0, fields_ref.at[:, depth - 1], state.at[:, 0], 0),
        halo(2, 1, fields_ref.at[:, 0], state.at[:, depth + 1], 1),
    ]
    z_second = [
        halo(2, 0, update.at[:, depth], update.at[:, 0], 2),
        halo(2, 1, update.at[:, 1], update.at[:, depth + 1], 3),
    ]
    xy_first = [
        halo(1, way, y_send.at[0, way], y_recv.at[0, way], 4 + way) for way in range(2)
    ] + [halo(0, way, x_send.at[0], x_recv.at[0, way], 6 + way) for way in range(2)]
    xy_second = [
        [
            halo(1, way, y_send.at[1, way, part], y_recv.at[1, way, part], 8 + 4 * part + way)
            for way in range(2)
        ]
        + [
            halo(0, way, x_send.at[1, part], x_recv.at[1, way, part], 10 + 4 * part + way)
            for way in range(2)
        ]
        for part in range(PARTS)
    ]
    every_halo = z_first + z_second + xy_first + xy_second[0] + xy_second[1]

    lane = lax.broadcasted_iota(jnp.int32, (span_cells, wind), 1)
    row = lax.broadcasted_iota(jnp.int32, (span_cells, wind), 0)
    lane_pair = lane >> 1

    def pack(stage, part, z, values, held_x):
        packed = list(held_x)
        for f in range(FIELDS):
            y_send[stage, 0, part, f, pl.ds(z, 1), :] = values[f][span_cells - 1 : span_cells, :]
            y_send[stage, 1, part, f, pl.ds(z, 1), :] = values[f][0:1, :]
            pair = (f % per_group) * half + z
            turned = pltpu.roll(values[f], 2 * pair + 1, 1)
            g = f // per_group
            packed[g] = jnp.where(lane_pair == pair, turned, packed[g])
        return tuple(packed)

    no_columns = tuple(jnp.zeros((span_cells, wind), jnp.float32) for _ in range(groups))

    load.wait()
    for part in range(PARTS):

        def pack_plane(z, held_x, part=part):
            values = [state[f, 1 + part * half + z] for f in range(FIELDS)]
            return pack(0, part, z, values, held_x)

        packed = lax.fori_loop(0, half, pack_plane, no_columns)
        for g in range(groups):
            x_send[0, part, g] = packed[g]

    pl.semaphore_wait(barrier, tiles - 1 + n_stream - 1)

    def spread(peers, count, src, dst, mine, send_sem, recv_sem):
        copies = []
        for step in range(1, count):
            peer, device = peers(step)
            copy = pltpu.make_async_remote_copy(
                src_ref=src(peer),
                dst_ref=dst.at[mine],
                send_sem=send_sem.at[peer],
                recv_sem=recv_sem.at[mine],
                device_id=device,
                device_id_type=MESH,
            )
            copy.start()
            arrival = pltpu.make_async_remote_copy(
                src_ref=src(peer),
                dst_ref=dst.at[peer],
                send_sem=send_sem.at[peer],
                recv_sem=recv_sem.at[peer],
                device_id=device,
                device_id_type=MESH,
            )
            copies.append((copy, arrival))
        return copies

    pan_copies = spread(
        tile_peer, tiles, lambda peer: pan_send.at[peer], pan_recv, my_tile, pan_s, pan_r
    )
    for start, _, _, clear in z_first + xy_first:
        start()
    for _, _, _, clear in every_halo:
        clear()
    pan_recv[my_tile] = pan_send[my_tile]

    total_z, total_y = depth * n_vert, span_cells * n_span
    period = total_y * total_z
    plane = depth * span_cells
    cell_z, cell_y = split_index(lax.broadcasted_iota(jnp.int32, (plane, spec), 0), span_cells)
    upward, across = split_index(lax.broadcasted_iota(jnp.int32, (plane, spec), 1), wave_cols)
    phase = across * (span_pos * span_cells + cell_y) * total_z
    phase = phase + upward * (vert_pos * depth + cell_z) * total_y
    phase = split_index(phase, period)[1]
    cosine, sine = circle(phase.astype(jnp.float32) * (1.0 / period))
    wave[:, 0:spec] = cosine
    wave[:, spec:] = sine

    for _, arrival in pan_copies:
        arrival.wait_recv()
    mine = pan_recv[0]
    for t in range(1, tiles):
        mine = mine + pan_recv[t]
    co_send[...] = mine
    co_copies = spread(
        stream_peer, n_stream, lambda peer: co_send, co_recv, stream_pos, co_s, co_r
    )
    co_recv[stream_pos] = mine

    for _, arrive, _, _ in z_first + xy_first:
        arrive()
    even = (lane & 1) == 0

    def columns(stage, part):
        for g in range(groups):
            from_low = pltpu.roll(x_recv[stage, 0, part, g], 1, 1)
            from_high = pltpu.roll(x_recv[stage, 1, part, g], wind - 1, 1)
            x_both[stage, part, g] = jnp.where(even, from_high, from_low)

    for part in range(PARTS):
        columns(0, part)

    for _, arrival in co_copies:
        arrival.wait_recv()
    coeffs = co_recv[0]
    for t in range(1, n_stream):
        coeffs = coeffs + co_recv[t]
    inflow = lax.dot_general(
        wave[...],
        coeffs,
        (((1,), (1,)), ((), ())),
        precision=HIGHEST,
        preferred_element_type=jnp.float32,
    )
    first_field = lax.broadcasted_iota(jnp.int32, inflow.shape, 1) == 0
    target[...] = inflow + jnp.where(first_field, 1.0, 0.0)

    spots = stream_pos * wind + lane
    relax = jnp.where(
        spots < wind // 2, jnp.exp(spots.astype(jnp.float32) * (-1.0 / relax_depth)) / relax_time, 0.0
    )
    relax_dt = time_step * relax
    diffusion = [viscous] * 4 + [heat_diff]
    keep = {nu: 1.0 - time_step * (6.0 * nu) - relax_dt for nu in set(diffusion)}
    half_dt = 0.5 * time_step

    def advance(source, stage, part, z):
        at = part * half + z
        wanted = target[pl.ds(pl.multiple_of(at * span_cells, span_cells), span_cells), :]
        centre = [source[f, 1 + at] for f in range(FIELDS)]
        u, v, w = (half_dt * centre[f] for f in range(3))
        diff_x, diff_y, diff_z, new = [], [], [], []
        for f in range(FIELDS):
            c = centre[f]
            pair = (f % per_group) * half + z
            side = pltpu.roll(x_both[stage, part, f // per_group], wind - 1 - 2 * pair, 1)
            west = jnp.where(lane == 0, side, pltpu.roll(c, 1, 1))
            east = jnp.where(lane == wind - 1, side, pltpu.roll(c, wind - 1, 1))
            low = jnp.broadcast_to(y_recv[stage, 0, part, f, pl.ds(z, 1), :], c.shape)
            high = jnp.broadcast_to(y_recv[stage, 1, part, f, pl.ds(z, 1), :], c.shape)
            south = jnp.where(row == 0, low, pltpu.roll(c, 1, 0))
            north = jnp.where(row == span_cells - 1, high, pltpu.roll(c, span_cells - 1, 0))
            lower = source[f, at]
            upper = source[f, at + 2]
            dx, dy, dz = east - west, north - south, upper - lower
            around = (east + west) + (north + south) + (upper + lower)
            nu = diffusion[f]
            value = keep[nu] * c + (time_step * nu) * around
            value = value + relax_dt * jnp.broadcast_to(wanted[:, f : f + 1], c.shape)
            value = value - (u * dx + v * dy + w * dz)
            diff_x.append(dx)
            diff_y.append(dy)
            diff_z.append(dz)
            new.append(value)
        damping = (2.0 / penalty) * solid_ref[at]
        new[0] = new[0] - half_dt * diff_x[3] - damping * u
        new[1] = new[1] - half_dt * diff_y[3] - damping * v
        new[2] = new[2] - half_dt * diff_z[3] - damping * w + (time_step * buoyant) * centre[4]
        new[3] = new[3] - (half_dt * sound_sq) * (diff_x[0] + diff_y[1] + diff_z[2])
        return new

    for part in range(PARTS):

        def first_plane(z, held_x, part=part):
            new = advance(state, 0, part, z)
            for f in range(FIELDS):
                update[f, 1 + part * half + z] = new[f]
            return pack(1, part, z, new, held_x)

        packed = lax.fori_loop(0, half, first_plane, no_columns)
        for g in range(groups):
            x_send[1, part, g] = packed[g]
        for start, _, _, _ in xy_second[part]:
            start()
        if part == 0:
            z_second[1][0]()
    z_second[0][0]()

    def second_plane(part, z):
        new = advance(update, 1, part, z)
        at = part * half + z
        for f in range(FIELDS):
            value = 0.5 * (state[f, 1 + at] + new[f])
            result[f, at] = value
            if f == 3:
                top = value.astype(jnp.bfloat16)
                rest = (value - top.astype(jnp.float32)).astype(jnp.bfloat16)
                where = pl.ds(pl.multiple_of(at * span_cells, span_cells), span_cells)
                press[where, 0:wind] = top
                press[where, wind:] = rest

    def store(part):
        where = pl.ds(part * half, half)
        return pltpu.make_async_copy(
            result.at[:, where], out_ref.at[:, where], local_sem.at[1 + part]
        )

    for part in range(PARTS):
        for _, arrive, _, _ in xy_second[part]:
            arrive()
        columns(1, part)
        if part == PARTS - 1:
            z_second[1][1]()

        def plane_step(z, carry, part=part):
            second_plane(part, z)
            return carry

        lax.fori_loop(1 if part == 0 else 0, half, plane_step, 0)
        if part == 0:
            z_second[0][1]()
            second_plane(0, 0)
        store(part).start()

    width = min(deck, 256)
    base = span_pos * strip_share
    hit_row = lax.broadcasted_iota(jnp.int32, (plane, width), 0)
    hit_col = lax.broadcasted_iota(jnp.int32, (wind, width), 0)

    def deck_step(i, totals):
        where = pl.ds(pl.multiple_of(i * width, width), width)
        cell_row, cell_col = split_index(cells_ref[0, 0, :, where], wind)
        pick = jnp.where(hit_col == cell_col, 1.0, 0.0).astype(jnp.bfloat16)
        pick = jnp.concatenate([pick, pick], axis=0)
        rows = jnp.dot(press[...], pick, preferred_element_type=jnp.float32)
        sampled = jnp.sum(jnp.where(hit_row == cell_row, rows, 0.0), axis=0, keepdims=True)
        traction = sampled * geom_ref[0, span_pos, 0, :, where]
        strip = strips_ref[0, span_pos, :, where]
        return tuple(
            total + jnp.where(strip == base + j, traction, 0.0) for j, total in enumerate(totals)
        )

    totals = lax.fori_loop(
        0,
        deck // width,
        deck_step,
        tuple(jnp.zeros((3, width), jnp.float32) for _ in range(strip_share)),
    )
    part_force = jnp.zeros((1, n_modes), jnp.float32)
    for j in range(strip_share):
        force = jnp.sum(totals[j], axis=1, keepdims=True)
        for c in range(3):
            part_force = part_force + force[c : c + 1, :] * modes_ref[c, pl.ds(base + j, 1), :]
    md_send[...] = jnp.zeros_like(md_send)
    md_send[0:1, 0:n_modes] = part_force
    md_copies = spread(tile_peer, tiles, lambda peer: md_send, md_recv, my_tile, md_s, md_r)
    md_recv[my_tile] = md_send[...]
    for _, arrival in md_copies:
        arrival.wait_recv()
    group_force = md_recv[0]
    for t in range(1, tiles):
        group_force = group_force + md_recv[t]
    sd_send[...] = group_force
    sd_copies = spread(
        stream_peer, n_stream, lambda peer: sd_send, sd_recv, stream_pos, sd_s, sd_r
    )
    sd_recv[stream_pos] = group_force
    for copy, _ in pan_copies + co_copies + md_copies:
        copy.wait_send()
    for _, _, leave, _ in every_halo:
        leave()
    for part in range(PARTS):
        store(part).wait()
    for _, arrival in sd_copies:
        arrival.wait_recv()
    force_all = sd_recv[0]
    for t in range(1, n_stream):
        force_all = force_all + sd_recv[t]
    modal_ref[...] = force_all[0:1, 0:n_modes]
    for copy, _ in sd_copies:
        copy.wait_send()


def on_device(sizes, fields, solid, panels, owner, cells, geom, strips, modes):
    n_stream, n_span, n_vert = sizes
    tiles = n_span * n_vert
    depth, span_cells, wind = fields.shape[1:]
    half = depth // PARTS
    per_group = min(FIELDS, (wind // 2) // half)
    groups = -(-FIELDS // per_group)
    spec_cols = panels.shape[2]
    n_modes = modes.shape[2]
    plane = depth * span_cells
    f32 = jnp.float32
    dma = pltpu.SemaphoreType.DMA
    vmem = pl.BlockSpec(memory_space=pltpu.VMEM)
    anywhere = pl.BlockSpec(memory_space=pl.ANY)
    new_fields, modal = pl.pallas_call(
        functools.partial(kernel, sizes),
        out_shape=(
            jax.ShapeDtypeStruct(fields.shape, f32),
            jax.ShapeDtypeStruct((1, n_modes), f32),
        ),
        in_specs=[anywhere] + [vmem] * 7,
        out_specs=(anywhere, vmem),
        scratch_shapes=[
            pltpu.VMEM((FIELDS, depth + 2, span_cells, wind), f32),
            pltpu.VMEM((FIELDS, depth + 2, span_cells, wind), f32),
            pltpu.VMEM((FIELDS, depth, span_cells, wind), f32),
            pltpu.VMEM((2, PARTS, groups, span_cells, wind), f32),
            pltpu.VMEM((2, 2, PARTS, groups, span_cells, wind), f32),
            pltpu.VMEM((2, PARTS, groups, span_cells, wind), f32),
            pltpu.VMEM((2, 2, PARTS, FIELDS, half, wind), f32),
            pltpu.VMEM((2, 2, PARTS, FIELDS, half, wind), f32),
            pltpu.VMEM((panels.shape[0], ROWS, spec_cols), f32),
            pltpu.VMEM((tiles, ROWS, spec_cols), f32),
            pltpu.VMEM((tiles, ROWS, spec_cols), f32),
            pltpu.VMEM((ROWS, spec_cols), f32),
            pltpu.VMEM((n_stream, ROWS, spec_cols), f32),
            pltpu.VMEM((plane, spec_cols), f32),
            pltpu.VMEM((plane, ROWS), f32),
            pltpu.VMEM((plane, 2 * wind), jnp.bfloat16),
            pltpu.VMEM((ROWS, 128), f32),
            pltpu.VMEM((tiles, ROWS, 128), f32),
            pltpu.VMEM((ROWS, 128), f32),
            pltpu.VMEM((n_stream, ROWS, 128), f32),
            dma((1 + PARTS,)),
            dma((8 + 4 * PARTS,)),
            dma((8 + 4 * PARTS,)),
            dma((tiles,)),
            dma((tiles,)),
            dma((n_stream,)),
            dma((n_stream,)),
            dma((tiles,)),
            dma((tiles,)),
            dma((n_stream,)),
            dma((n_stream,)),
        ],
        compiler_params=pltpu.CompilerParams(
            collective_id=0, has_side_effects=True, vmem_limit_bytes=48 * 1024 * 1024
        ),
        name="wind_steps",
    )(fields, solid, panels, owner, cells, geom, strips, modes)
    return new_fields, modal[0]


def solution(mesh):
    sizes = tuple(mesh.shape[axis] for axis in ("stream", "span", "vert"))
    return jax.shard_map(
        functools.partial(on_device, sizes),
        mesh=mesh,
        in_specs=(
            P(None, "vert", "span", "stream"),
            P("vert", "span", "stream"),
            P(("stream", "span", "vert"), None, None),
            P(("stream", "span", "vert"), None),
            P("vert", "span", "stream", None),
            P("vert", None, "stream", None, None),
            P("vert", None, "stream", None),
            P(),
        ),
        out_specs=(P(None, "vert", "span", "stream"), P()),
        check_vma=False,
    )
```

time: 157 us -> 46.4 us (0.30)
  starting transfers between devices: 40.1 us -> 0 us
  blocking collectives: 39.9 us -> 0 us
  Pallas kernels: 0 us -> 36.6 us
  other arithmetic: 35.2 us -> 0 us
  local copies, waits for them, and re-layouts: 29.5 us -> 8.64 us
  waiting for transfers between devices: 6.79 us -> 0 us
  matrix products: 3.25 us -> 0 us
    pallas_call x0 -> x1, Pallas kernels: none -> 36.6 us  [on_device(): pl.pallas_call(functools.partial(kernel, sizes), out_shape=(jax.ShapeDtyp...]
    ppermute x12 -> x0, starting transfers between devices: 33.1 us -> none  [the longest x6 25.1 us: extended(): lax.ppermute(lax.slice_in_dim(block, block.shape[dim] - width, None, axis...]
    psum x2 -> x0, blocking collectives: 25.4 us -> none  [the longest x1 17.7 us: on_device(): modal_force = lax.psum(modal_part, ('stream', 'vert'))]
    mul x10 -> x0, other arithmetic: 14.8 us -> none  [the longest x2 6.36 us: rates(): grad_z = 0.5 * (upper_side - lower_side)]
    all_gather x1 -> x0, blocking collectives: 14.5 us -> none  [on_device(): lax.all_gather(sampled.reshape(1, 1, 1, -1), 'span', axis=1, tiled=True)]
    gather x1 -> x0, local copies, waits for them, and re-layouts: 11.8 us -> none  [on_device(): sampled = pressure[deck_cells[0, 0, 0]]]
    add x6 -> x0, other arithmetic: 7.95 us -> none  [the longest x1 7.84 us: on_device(): first_update = fields + time_step * advance(fields)]
    slice x5 -> x0, local copies, waits for them, and re-layouts: 7.92 us -> none  [the longest x3 6.01 us: extended(): lax.slice_in_dim(block, block.shape[dim] - width, None, axis=dim)]
  transfers between devices with their start and end apart: 13 -> 0, of which waited for: 4 -> 0; matrix products, arithmetic and copies ran while one was open for 14% -> 0% of each run, Pallas kernels for 0% -> 0%
where the time goes in v1:
time: 46.4 us; the launch traced here: 45.9 us
  Pallas kernels  36.6 us (79%)
  local copies, waits for them, and re-layouts  8.64 us (19%)
  between operations  0.66 us (1%)
    pallas_call x1, Pallas kernels, on_device(): pl.pallas_call(functools.partial(kernel, sizes), out_shape=(jax.ShapeDtyp...  36.6 us
    unnamed x15, local copies, waits for them, and re-layouts  8.64 us

profile of v1, /device:TPU:0, one launch (start us, length us, event | category | flops | bytes accessed | tf_op | source)
XLA Modules:
  0.0 45.9 jit_solution(11361194964193878336)
XLA Ops:
  0.6 0.7 %copy.11.owner_ref = s32[16,1]{1,0:T(8,128)S(1)} copy(s32[16,1]{0,1:T(1,128)} %param.11) | data formatting | bytes 128 | tf_op args[3]
  1.4 0.9 %copy.10.panels_ref = f32[16,5,256]{2,1,0:T(8,128)S(1)} copy(f32[16,5,256]{2,0,1:T(8,128)} %param.10) | data formatting | bytes 163840 | tf_op args[2]
  2.3 0.9 %copy.12.geom_ref = f32[1,4,1,3,2048]{4,3,2,1,0:T(4,128)S(1)} copy(f32[1,4,1,3,2048]{4,2,3,1,0:T(1,128)} %param.13) | data formatting | bytes 196608 | tf_op args[5]
  3.3 0.0 copy-start
  3.3 1.3 %copy-done = f32[5,32,16,128]{3,2,1,0:T(8,128)S(1)} copy-done((f32[5,32,16,128]{3,2,1,0:T(8,128)S(1)}, f32[5,32,16,128]{3,2,1,0:T(8,128)}, u32[]{:S(2)}) %copy-start) | copy-done | bytes 1310744
  4.6 0.0 copy-start.1
  4.6 0.9 %copy-done.1 = f32[32,16,128]{2,1,0:T(8,128)S(1)} copy-done((f32[32,16,128]{2,1,0:T(8,128)S(1)}, f32[32,16,128]{2,1,0:T(8,128)}, u32[]{:S(2)}) %copy-start.1) | copy-done | bytes 262168
  5.5 0.0 copy-start.2
  5.5 0.8 %copy-done.2 = s32[1,4,1,2048]{3,2,1,0:T(1,128)S(1)} copy-done((s32[1,4,1,2048]{3,2,1,0:T(1,128)S(1)}, s32[1,4,1,2048]{3,2,1,0:T(1,128)}, u32[]{:S(2)}) %copy-start.2) | copy-done | bytes 32792
  6.3 0.0 copy-start.3
  6.3 0.7 %copy-done.3 = f32[3,16,32]{2,1,0:T(8,128)S(1)} copy-done((f32[3,16,32]{2,1,0:T(8,128)S(1)}, f32[3,16,32]{2,1,0:T(8,128)}, u32[]{:S(2)}) %copy-start.3) | copy-done | bytes 6168
  7.0 0.0 copy-start.4
  7.0 0.7 %copy-done.4 = s32[1,1,1,2048]{3,2,1,0:T(1,128)S(1)} copy-done((s32[1,1,1,2048]{3,2,1,0:T(1,128)S(1)}, s32[1,1,1,2048]{3,2,1,0:T(1,128)}, u32[]{:S(2)}) %copy-start.4) | copy-done | bytes 8216
  7.7 36.6 %wind_steps.1 = (f32[5,32,16,128]{3,2,1,0:T(8,128)S(1)}, f32[1,32]{1,0:T(1,128)S(1)}) custom-call(f32[5,32,16,128]{3,2,1,0:T(8,128)S(1)} %copy-done, f32[32,16,128]{2,1,0:T(8,128)S(1)} %copy-done.1, f32[16,5,256]{2,1,0:T(8,128)S(1)} %copy.10.panels_ref, s32[16,1]{1,0:T(8,128)S(1)} %copy.11.owner_ref, s32[1,1,1,2048]{3,2,1,0:T(1,128)S(1)} %copy-done.4, ...), custom_call_target="tpu_custom_call" | custom-call | tf_op jit(solution)/shard_map/wind_steps/pallas_call | solution.py:488
  44.4 1.1 %copy.15 = f32[5,32,16,128]{3,2,1,0:T(8,128)} copy(f32[5,32,16,128]{3,2,1,0:T(8,128)S(1)} %get-tuple-element.8) | data formatting | bytes 2621440
  45.4 0.5 %copy.16 = f32[32]{0:T(128)} copy(f32[32]{0:T(128)S(1)} %bitcast.1) | data formatting | bytes 256
Async XLA Ops:
  3.3 1.3 %copy-start = (f32[5,32,16,128]{3,2,1,0:T(8,128)S(1)}, f32[5,32,16,128]{3,2,1,0:T(8,128)}, u32[]{:S(2)}) copy-start(f32[5,32,16,128]{3,2,1,0:T(8,128)} %fields_ref.1) | copy-start | bytes 3932164
  4.6 0.9 %copy-start.1 = (f32[32,16,128]{2,1,0:T(8,128)S(1)}, f32[32,16,128]{2,1,0:T(8,128)}, u32[]{:S(2)}) copy-start(f32[32,16,128]{2,1,0:T(8,128)} %solid_ref.1) | copy-start | bytes 786436
  5.5 0.8 %copy-start.2 = (s32[1,4,1,2048]{3,2,1,0:T(1,128)S(1)}, s32[1,4,1,2048]{3,2,1,0:T(1,128)}, u32[]{:S(2)}) copy-start(s32[1,4,1,2048]{3,2,1,0:T(1,128)} %strips_ref.1) | copy-start | bytes 98308
  6.3 0.7 %copy-start.3 = (f32[3,16,32]{2,1,0:T(8,128)S(1)}, f32[3,16,32]{2,1,0:T(8,128)}, u32[]{:S(2)}) copy-start(f32[3,16,32]{2,1,0:T(8,128)} %modes_ref.1) | copy-start | bytes 18436
  7.0 0.7 %copy-start.4 = (s32[1,1,1,2048]{3,2,1,0:T(1,128)S(1)}, s32[1,1,1,2048]{3,2,1,0:T(1,128)}, u32[]{:S(2)}) copy-start(s32[1,1,1,2048]{3,2,1,0:T(1,128)} %cells_ref.1) | copy-start | bytes 24580

commit v2 on v1

--- a/solution.py
+++ b/solution.py
@@ -21,8 +21,8 @@
 relax_depth = 8.0
 wave_cols = 16
 FIELDS = 5
-ROWS = 8
 PARTS = 2
+ONE_HOP = 64
 
 
 def split_index(values, size):
@@ -63,6 +63,12 @@
     state,
     update,
     result,
+    solid_in,
+    owner_in,
+    cells_in,
+    geom_in,
+    strips_in,
+    modes_in,
     x_send,
     x_recv,
     x_both,
@@ -73,12 +79,12 @@
     pan_recv,
     co_send,
     co_recv,
+    co_rows,
     wave,
     target,
     press,
     md_send,
     md_recv,
-    sd_send,
     sd_recv,
     local_sem,
     halo_s,
@@ -98,7 +104,7 @@
     half = depth // PARTS
     per_group = min(FIELDS, (wind // 2) // half)
     groups = -(-FIELDS // per_group)
-    held = panels_ref.shape[0]
+    held = panels_ref.shape[1]
     spec_cols = panels_ref.shape[2]
     spec = spec_cols // 2
     strip_share = modes_ref.shape[1] // n_span
@@ -117,31 +123,54 @@
         peer = lax.rem(stream_pos + step, n_stream)
         return peer, (peer, span_pos, vert_pos)
 
-    load = pltpu.make_async_copy(fields_ref, state.at[:, pl.ds(1, depth)], local_sem.at[0])
-    load.start()
-
+    def any_peer(step):
+        peer = lax.rem(stream_pos * tiles + my_tile + step, n_stream * tiles)
+        stream = lax.div(peer, jnp.int32(tiles))
+        rest = peer - stream * tiles
+        whole = lax.div(rest, jnp.int32(n_vert))
+        return peer, (stream, whole, rest - whole * n_vert)
+
+    one_hop = n_stream * tiles <= ONE_HOP
+    if one_hop:
+        meets = [(any_peer, n_stream * tiles)]
+        hops = [(any_peer, n_stream * tiles, stream_pos * tiles + my_tile)]
+    else:
+        meets = [(tile_peer, tiles), (stream_peer, n_stream)]
+        hops = [(tile_peer, tiles, my_tile), (stream_peer, n_stream, stream_pos)]
     barrier = pltpu.get_barrier_semaphore()
-    for step in range(1, tiles):
-        pl.semaphore_signal(barrier, inc=1, device_id=tile_peer(step)[1], device_id_type=MESH)
-    for step in range(1, n_stream):
-        pl.semaphore_signal(barrier, inc=1, device_id=stream_peer(step)[1], device_id_type=MESH)
-
-    pan_in[...] = jnp.zeros_like(pan_in)
-    pan_in[:, 0:FIELDS, :] = panels_ref[...]
-    owner = jnp.broadcast_to(owner_ref[...], (held, tiles * ROWS))
-    owner = jnp.broadcast_to(owner[:, None, :], (held, ROWS, tiles * ROWS))
-    owner = owner.reshape(held * ROWS, tiles * ROWS)
-    row_field = lax.broadcasted_iota(jnp.int32, owner.shape, 0) & (ROWS - 1)
-    col_tile, col_field = split_index(lax.broadcasted_iota(jnp.int32, owner.shape, 1), ROWS)
-    route = jnp.where((owner == col_tile) & (row_field == col_field), 1.0, 0.0)
-    sums = lax.dot_general(
-        route,
-        pan_in[...].reshape(held * ROWS, spec_cols),
-        (((0,), (0,)), ((), ())),
-        precision=HIGHEST,
-        preferred_element_type=jnp.float32,
-    )
-    pan_send[...] = sums.reshape(tiles, ROWS, spec_cols)
+    for peers, count in meets:
+        for step in range(1, count):
+            pl.semaphore_signal(barrier, inc=1, device_id=peers(step)[1], device_id_type=MESH)
+
+    loads = [
+        pltpu.make_async_copy(src, dst, local_sem.at[i])
+        for i, (src, dst) in enumerate(
+            [
+                (panels_ref, pan_in),
+                (owner_ref, owner_in),
+                (fields_ref, state.at[:, pl.ds(1, depth)]),
+                (solid_ref, solid_in),
+                (cells_ref, cells_in),
+                (geom_ref.at[0, span_pos], geom_in),
+                (strips_ref.at[0, span_pos], strips_in),
+                (modes_ref, modes_in),
+            ]
+        )
+    ]
+    for load in loads:
+        load.start()
+
+    loads[0].wait()
+    loads[1].wait()
+    owner = jnp.broadcast_to(owner_in[...], (tiles, held))
+    wanted_by = lax.broadcasted_iota(jnp.int32, (tiles, held), 0)
+    route = jnp.where(owner == wanted_by, 1.0, 0.0)
+    for f in range(FIELDS):
+        sums = jnp.dot(
+            route, pan_in[f], precision=HIGHEST, preferred_element_type=jnp.float32
+        )
+        for t in range(tiles):
+            pan_send[t, :, f * spec_cols : (f + 1) * spec_cols] = sums[t : t + 1, :]
 
     def halo(axis, way, src, dst, sem):
         count, place = sizes[axis], me[axis]
@@ -218,18 +247,7 @@
 
     no_columns = tuple(jnp.zeros((span_cells, wind), jnp.float32) for _ in range(groups))
 
-    load.wait()
-    for part in range(PARTS):
-
-        def pack_plane(z, held_x, part=part):
-            values = [state[f, 1 + part * half + z] for f in range(FIELDS)]
-            return pack(0, part, z, values, held_x)
-
-        packed = lax.fori_loop(0, half, pack_plane, no_columns)
-        for g in range(groups):
-            x_send[0, part, g] = packed[g]
-
-    pl.semaphore_wait(barrier, tiles - 1 + n_stream - 1)
+    pl.semaphore_wait(barrier, sum(count - 1 for _, count in meets))
 
     def spread(peers, count, src, dst, mine, send_sem, recv_sem):
         copies = []
@@ -258,11 +276,24 @@
     pan_copies = spread(
         tile_peer, tiles, lambda peer: pan_send.at[peer], pan_recv, my_tile, pan_s, pan_r
     )
-    for start, _, _, clear in z_first + xy_first:
+    for start, _, _, _ in z_first:
         start()
+    pan_recv[my_tile] = pan_send[my_tile]
     for _, _, _, clear in every_halo:
         clear()
-    pan_recv[my_tile] = pan_send[my_tile]
+
+    loads[2].wait()
+    for part in range(PARTS):
+
+        def pack_plane(z, held_x, part=part):
+            values = [state[f, 1 + part * half + z] for f in range(FIELDS)]
+            return pack(0, part, z, values, held_x)
+
+        packed = lax.fori_loop(0, half, pack_plane, no_columns, unroll=4)
+        for g in range(groups):
+            x_send[0, part, g] = packed[g]
+    for start, _, _, _ in xy_first:
+        start()
 
     total_z, total_y = depth * n_vert, span_cells * n_span
     period = total_y * total_z
@@ -273,19 +304,12 @@
     phase = phase + upward * (vert_pos * depth + cell_z) * total_y
     phase = split_index(phase, period)[1]
     cosine, sine = circle(phase.astype(jnp.float32) * (1.0 / period))
-    wave[:, 0:spec] = cosine
-    wave[:, spec:] = sine
-
-    for _, arrival in pan_copies:
-        arrival.wait_recv()
-    mine = pan_recv[0]
-    for t in range(1, tiles):
-        mine = mine + pan_recv[t]
-    co_send[...] = mine
-    co_copies = spread(
-        stream_peer, n_stream, lambda peer: co_send, co_recv, stream_pos, co_s, co_r
-    )
-    co_recv[stream_pos] = mine
+    for i, values in enumerate((cosine, sine)):
+        top = values.astype(jnp.bfloat16)
+        rest = (values - top.astype(jnp.float32)).astype(jnp.bfloat16)
+        wave[:, i * spec : (i + 1) * spec] = top
+        wave[:, spec_cols + i * spec : spec_cols + (i + 1) * spec] = top
+        wave[:, 2 * spec_cols + i * spec : 2 * spec_cols + (i + 1) * spec] = rest
 
     for _, arrive, _, _ in z_first + xy_first:
         arrive()
@@ -300,21 +324,6 @@
     for part in range(PARTS):
         columns(0, part)
 
-    for _, arrival in co_copies:
-        arrival.wait_recv()
-    coeffs = co_recv[0]
-    for t in range(1, n_stream):
-        coeffs = coeffs + co_recv[t]
-    inflow = lax.dot_general(
-        wave[...],
-        coeffs,
-        (((1,), (1,)), ((), ())),
-        precision=HIGHEST,
-        preferred_element_type=jnp.float32,
-    )
-    first_field = lax.broadcasted_iota(jnp.int32, inflow.shape, 1) == 0
-    target[...] = inflow + jnp.where(first_field, 1.0, 0.0)
-
     spots = stream_pos * wind + lane
     relax = jnp.where(
         spots < wind // 2, jnp.exp(spots.astype(jnp.float32) * (-1.0 / relax_depth)) / relax_time, 0.0
@@ -324,9 +333,16 @@
     keep = {nu: 1.0 - time_step * (6.0 * nu) - relax_dt for nu in set(diffusion)}
     half_dt = 0.5 * time_step
 
-    def advance(source, stage, part, z):
+    def inflow_term(at):
+        wanted = target[pl.ds(pl.multiple_of(at * span_cells, span_cells), span_cells), :]
+        return [
+            relax_dt * jnp.broadcast_to(wanted[:, f : f + 1], (span_cells, wind))
+            for f in range(FIELDS)
+        ]
+
+    def advance(source, stage, part, z, inflow=True):
         at = part * half + z
-        wanted = target[pl.ds(pl.multiple_of(at * span_cells, span_cells), span_cells), :]
+        terms = inflow_term(at) if inflow else None
         centre = [source[f, 1 + at] for f in range(FIELDS)]
         u, v, w = (half_dt * centre[f] for f in range(3))
         diff_x, diff_y, diff_z, new = [], [], [], []
@@ -346,35 +362,82 @@
             around = (east + west) + (north + south) + (upper + lower)
             nu = diffusion[f]
             value = keep[nu] * c + (time_step * nu) * around
-            value = value + relax_dt * jnp.broadcast_to(wanted[:, f : f + 1], c.shape)
+            if inflow:
+                value = value + terms[f]
             value = value - (u * dx + v * dy + w * dz)
             diff_x.append(dx)
             diff_y.append(dy)
             diff_z.append(dz)
             new.append(value)
-        damping = (2.0 / penalty) * solid_ref[at]
+        damping = (2.0 / penalty) * solid_in[at]
         new[0] = new[0] - half_dt * diff_x[3] - damping * u
         new[1] = new[1] - half_dt * diff_y[3] - damping * v
         new[2] = new[2] - half_dt * diff_z[3] - damping * w + (time_step * buoyant) * centre[4]
         new[3] = new[3] - (half_dt * sound_sq) * (diff_x[0] + diff_y[1] + diff_z[2])
         return new
 
-    for part in range(PARTS):
-
-        def first_plane(z, held_x, part=part):
-            new = advance(state, 0, part, z)
-            for f in range(FIELDS):
-                update[f, 1 + part * half + z] = new[f]
-            return pack(1, part, z, new, held_x)
-
-        packed = lax.fori_loop(0, half, first_plane, no_columns)
+    loads[3].wait()
+
+    def plain_plane(z, carry):
+        new = advance(state, 0, 0, z, inflow=False)
+        for f in range(FIELDS):
+            update[f, 1 + z] = new[f]
+        return carry
+
+    lax.fori_loop(0, half // 2, plain_plane, 0, unroll=2)
+
+    for _, arrival in pan_copies:
+        arrival.wait_recv()
+    mine = pan_recv[0]
+    for t in range(1, tiles):
+        mine = mine + pan_recv[t]
+    co_send[...] = mine
+    co_copies = spread(
+        stream_peer, n_stream, lambda peer: co_send, co_recv, stream_pos, co_s, co_r
+    )
+    co_recv[stream_pos] = mine
+
+    lax.fori_loop(half // 2, half, plain_plane, 0, unroll=2)
+
+    for _, arrival in co_copies:
+        arrival.wait_recv()
+    coeffs = co_recv[0]
+    for t in range(1, n_stream):
+        coeffs = coeffs + co_recv[t]
+    co_rows[...] = jnp.zeros_like(co_rows)
+    for f in range(FIELDS):
+        co_rows[f : f + 1, :] = coeffs[:, f * spec_cols : (f + 1) * spec_cols]
+    top = co_rows[...].astype(jnp.bfloat16)
+    rest = (co_rows[...] - top.astype(jnp.float32)).astype(jnp.bfloat16)
+    inflow = lax.dot_general(
+        wave[...],
+        jnp.concatenate([top, rest, top], axis=1),
+        (((1,), (1,)), ((), ())),
+        preferred_element_type=jnp.float32,
+    )
+    first_field = lax.broadcasted_iota(jnp.int32, inflow.shape, 1) == 0
+    target[...] = inflow + jnp.where(first_field, 1.0, 0.0)
+
+    def finish_plane(z, held_x):
+        terms = inflow_term(z)
+        new = [update[f, 1 + z] + terms[f] for f in range(FIELDS)]
+        for f in range(FIELDS):
+            update[f, 1 + z] = new[f]
+        return pack(1, 0, z, new, held_x)
+
+    def first_plane(z, held_x):
+        new = advance(state, 0, 1, z)
+        for f in range(FIELDS):
+            update[f, 1 + half + z] = new[f]
+        return pack(1, 1, z, new, held_x)
+
+    for part, (step_plane, turns) in enumerate(((finish_plane, 4), (first_plane, 2))):
+        packed = lax.fori_loop(0, half, step_plane, no_columns, unroll=turns)
         for g in range(groups):
             x_send[1, part, g] = packed[g]
         for start, _, _, _ in xy_second[part]:
             start()
-        if part == 0:
-            z_second[1][0]()
-    z_second[0][0]()
+        z_second[1 - part][0]()
 
     def second_plane(part, z):
         new = advance(update, 1, part, z)
@@ -392,7 +455,7 @@
     def store(part):
         where = pl.ds(part * half, half)
         return pltpu.make_async_copy(
-            result.at[:, where], out_ref.at[:, where], local_sem.at[1 + part]
+            result.at[:, where], out_ref.at[:, where], local_sem.at[8 + part]
         )
 
     for part in range(PARTS):
@@ -406,12 +469,17 @@
             second_plane(part, z)
             return carry
 
-        lax.fori_loop(1 if part == 0 else 0, half, plane_step, 0)
         if part == 0:
+            lax.fori_loop(2, half, plane_step, 0, unroll=2)
             z_second[0][1]()
             second_plane(0, 0)
+            second_plane(0, 1)
+        else:
+            lax.fori_loop(0, half, plane_step, 0, unroll=2)
         store(part).start()
 
+    for load in loads[4:]:
+        load.wait()
     width = min(deck, 256)
     base = span_pos * strip_share
     hit_row = lax.broadcasted_iota(jnp.int32, (plane, width), 0)
@@ -419,55 +487,56 @@
 
     def deck_step(i, totals):
         where = pl.ds(pl.multiple_of(i * width, width), width)
-        cell_row, cell_col = split_index(cells_ref[0, 0, :, where], wind)
+        cell_row, cell_col = split_index(cells_in[0, 0, :, where], wind)
         pick = jnp.where(hit_col == cell_col, 1.0, 0.0).astype(jnp.bfloat16)
         pick = jnp.concatenate([pick, pick], axis=0)
         rows = jnp.dot(press[...], pick, preferred_element_type=jnp.float32)
         sampled = jnp.sum(jnp.where(hit_row == cell_row, rows, 0.0), axis=0, keepdims=True)
-        traction = sampled * geom_ref[0, span_pos, 0, :, where]
-        strip = strips_ref[0, span_pos, :, where]
+        traction = [sampled * geom_in[c, :, where] for c in range(3)]
+        strip = strips_in[:, where]
         return tuple(
-            total + jnp.where(strip == base + j, traction, 0.0) for j, total in enumerate(totals)
+            total + jnp.where(strip == base + n // 3, traction[n % 3], 0.0)
+            for n, total in enumerate(totals)
         )
 
     totals = lax.fori_loop(
         0,
         deck // width,
         deck_step,
-        tuple(jnp.zeros((3, width), jnp.float32) for _ in range(strip_share)),
-    )
-    part_force = jnp.zeros((1, n_modes), jnp.float32)
-    for j in range(strip_share):
-        force = jnp.sum(totals[j], axis=1, keepdims=True)
-        for c in range(3):
-            part_force = part_force + force[c : c + 1, :] * modes_ref[c, pl.ds(base + j, 1), :]
-    md_send[...] = jnp.zeros_like(md_send)
-    md_send[0:1, 0:n_modes] = part_force
-    md_copies = spread(tile_peer, tiles, lambda peer: md_send, md_recv, my_tile, md_s, md_r)
-    md_recv[my_tile] = md_send[...]
-    for _, arrival in md_copies:
-        arrival.wait_recv()
-    group_force = md_recv[0]
-    for t in range(1, tiles):
-        group_force = group_force + md_recv[t]
-    sd_send[...] = group_force
-    sd_copies = spread(
-        stream_peer, n_stream, lambda peer: sd_send, sd_recv, stream_pos, sd_s, sd_r
-    )
-    sd_recv[stream_pos] = group_force
-    for copy, _ in pan_copies + co_copies + md_copies:
-        copy.wait_send()
-    for _, _, leave, _ in every_halo:
-        leave()
-    for part in range(PARTS):
-        store(part).wait()
-    for _, arrival in sd_copies:
-        arrival.wait_recv()
-    force_all = sd_recv[0]
-    for t in range(1, n_stream):
-        force_all = force_all + sd_recv[t]
-    modal_ref[...] = force_all[0:1, 0:n_modes]
-    for copy, _ in sd_copies:
+        tuple(jnp.zeros((1, width), jnp.float32) for _ in range(3 * strip_share)),
+        unroll=2,
+    )
+    force = jnp.sum(jnp.concatenate(totals, axis=0), axis=1, keepdims=True)
+    shapes = jnp.concatenate(
+        [modes_in[n % 3, pl.ds(base + n // 3, 1), :] for n in range(3 * strip_share)], axis=0
+    )
+    part_force = jnp.sum(force * shapes, axis=0, keepdims=True)
+    md_copies = []
+    slots = ((md_recv, md_s, md_r), (sd_recv, sd_s, sd_r))
+    for hop, (peers, count, mine) in enumerate(hops):
+        recv, send_sem, recv_sem = slots[hop]
+        md_send[hop] = jnp.zeros(md_send.shape[1:], jnp.float32)
+        md_send[hop, :, 0:n_modes] = part_force
+        copies = spread(
+            peers, count, lambda peer, hop=hop: md_send.at[hop], recv, mine, send_sem, recv_sem
+        )
+        recv[mine] = md_send[hop]
+        if hop == 0:
+            for copy, _ in pan_copies + co_copies:
+                copy.wait_send()
+            for _, _, leave, _ in every_halo:
+                leave()
+            for part in range(PARTS):
+                store(part).wait()
+        for _, arrival in copies:
+            arrival.wait_recv()
+        total = recv[0]
+        for t in range(1, count):
+            total = total + recv[t]
+        part_force = total[:, 0:n_modes]
+        md_copies = md_copies + copies
+    modal_ref[...] = part_force
+    for copy, _ in md_copies:
         copy.wait_send()
 
 
@@ -484,50 +553,64 @@
     f32 = jnp.float32
     dma = pltpu.SemaphoreType.DMA
     vmem = pl.BlockSpec(memory_space=pltpu.VMEM)
-    anywhere = pl.BlockSpec(memory_space=pl.ANY)
+    hbm = pl.BlockSpec(memory_space=pltpu.HBM)
+    held = panels.shape[0]
+    if n_stream * tiles <= ONE_HOP:
+        first_hop, second_hop = n_stream * tiles, 1
+    else:
+        first_hop, second_hop = tiles, n_stream
+    panels = panels.transpose(1, 0, 2)
+    owner = owner.reshape(1, held)
+    geom = geom.transpose(0, 1, 3, 2, 4)
     new_fields, modal = pl.pallas_call(
         functools.partial(kernel, sizes),
         out_shape=(
             jax.ShapeDtypeStruct(fields.shape, f32),
             jax.ShapeDtypeStruct((1, n_modes), f32),
         ),
-        in_specs=[anywhere] + [vmem] * 7,
-        out_specs=(anywhere, vmem),
+        in_specs=[hbm] * 8,
+        out_specs=(hbm, vmem),
         scratch_shapes=[
             pltpu.VMEM((FIELDS, depth + 2, span_cells, wind), f32),
             pltpu.VMEM((FIELDS, depth + 2, span_cells, wind), f32),
             pltpu.VMEM((FIELDS, depth, span_cells, wind), f32),
+            pltpu.VMEM(solid.shape, f32),
+            pltpu.VMEM(owner.shape, jnp.int32),
+            pltpu.VMEM(cells.shape, jnp.int32),
+            pltpu.VMEM(geom.shape[2:], f32),
+            pltpu.VMEM(strips.shape[2:], jnp.int32),
+            pltpu.VMEM(modes.shape, f32),
             pltpu.VMEM((2, PARTS, groups, span_cells, wind), f32),
             pltpu.VMEM((2, 2, PARTS, groups, span_cells, wind), f32),
             pltpu.VMEM((2, PARTS, groups, span_cells, wind), f32),
             pltpu.VMEM((2, 2, PARTS, FIELDS, half, wind), f32),
             pltpu.VMEM((2, 2, PARTS, FIELDS, half, wind), f32),
-            pltpu.VMEM((panels.shape[0], ROWS, spec_cols), f32),
-            pltpu.VMEM((tiles, ROWS, spec_cols), f32),
-            pltpu.VMEM((tiles, ROWS, spec_cols), f32),
-            pltpu.VMEM((ROWS, spec_cols), f32),
-            pltpu.VMEM((n_stream, ROWS, spec_cols), f32),
-            pltpu.VMEM((plane, spec_cols), f32),
-            pltpu.VMEM((plane, ROWS), f32),
+            pltpu.VMEM(panels.shape, f32),
+            pltpu.VMEM((tiles, 1, FIELDS * spec_cols), f32),
+            pltpu.VMEM((tiles, 1, FIELDS * spec_cols), f32),
+            pltpu.VMEM((1, FIELDS * spec_cols), f32),
+            pltpu.VMEM((n_stream, 1, FIELDS * spec_cols), f32),
+            pltpu.VMEM((16, spec_cols), f32),
+            pltpu.VMEM((plane, 3 * spec_cols), jnp.bfloat16),
+            pltpu.VMEM((plane, 16), f32),
             pltpu.VMEM((plane, 2 * wind), jnp.bfloat16),
-            pltpu.VMEM((ROWS, 128), f32),
-            pltpu.VMEM((tiles, ROWS, 128), f32),
-            pltpu.VMEM((ROWS, 128), f32),
-            pltpu.VMEM((n_stream, ROWS, 128), f32),
-            dma((1 + PARTS,)),
+            pltpu.VMEM((2, 1, 128), f32),
+            pltpu.VMEM((first_hop, 1, 128), f32),
+            pltpu.VMEM((second_hop, 1, 128), f32),
+            dma((8 + PARTS,)),
             dma((8 + 4 * PARTS,)),
             dma((8 + 4 * PARTS,)),
             dma((tiles,)),
             dma((tiles,)),
             dma((n_stream,)),
             dma((n_stream,)),
-            dma((tiles,)),
-            dma((tiles,)),
-            dma((n_stream,)),
-            dma((n_stream,)),
+            dma((first_hop,)),
+            dma((first_hop,)),
+            dma((second_hop,)),
+            dma((second_hop,)),
         ],
         compiler_params=pltpu.CompilerParams(
-            collective_id=0, has_side_effects=True, vmem_limit_bytes=48 * 1024 * 1024
+            collective_id=0, has_side_effects=True, vmem_limit_bytes=63 * 1024 * 1024
         ),
         name="wind_steps",
     )(fields, solid, panels, owner, cells, geom, strips, modes)

time: 46.4 us -> 34.4 us (0.74)
  Pallas kernels: 36.6 us -> 30.6 us
  local copies, waits for them, and re-layouts: 8.64 us -> 3.02 us
    pallas_call x1, Pallas kernels: 36.6 us -> 30.6 us  [on_device(): pl.pallas_call(functools.partial(kernel, sizes), out_shape=(jax.ShapeDtyp...]
    unnamed x15 -> x4, local copies, waits for them, and re-layouts: 8.64 us -> 3.02 us
where the time goes in v2:
time: 34.4 us; the launch traced here: 34.3 us
  Pallas kernels  30.6 us (89%)
  local copies, waits for them, and re-layouts  3.02 us (9%)
  between operations  0.65 us (2%)
    pallas_call x1, Pallas kernels, on_device(): pl.pallas_call(functools.partial(kernel, sizes), out_shape=(jax.ShapeDtyp...  30.6 us
    unnamed x4, local copies, waits for them, and re-layouts  3.02 us

profile of v2, /device:TPU:0, one launch (start us, length us, event | category | flops | bytes accessed | tf_op | source)
XLA Modules:
  0.0 34.3 jit_solution(16838850261231896719)
XLA Ops:
  0.6 30.6 %wind_steps.1 = (f32[5,32,16,128]{3,2,1,0:T(8,128)}, f32[1,32]{1,0:T(1,128)}) custom-call(f32[5,32,16,128]{3,2,1,0:T(8,128)} %fields_ref.1, f32[32,16,128]{2,1,0:T(8,128)} %solid_ref.1, f32[5,16,256]{2,1,0:T(8,128)} %bitcast.5, s32[1,16]{1,0:T(1,128)} %bitcast.6, s32[1,1,1,2048]{3,2,1,0:T(1,128)} %cells_ref.1, f32[1,4,3,1,2048]{4,3,2,1,0:T(1,128)} %bitcast.4, ...), custom_call_target="tpu_custom_call" | custom-call | tf_op jit(solution)/shard_map/wind_steps/pallas_call | solution.py:565
  31.2 0.0 copy-start
  31.2 2.5 %copy.12 = f32[5,32,16,128]{3,2,1,0:T(8,128)} copy(f32[5,32,16,128]{3,2,1,0:T(8,128)} %get-tuple-element.8) | data formatting | bytes 2621440
  33.7 0.0 copy-done
  33.7 0.5 %copy.13 = f32[32]{0:T(128)} copy(f32[32]{0:T(128)S(1)} %bitcast.7) | data formatting | bytes 256
Async XLA Ops:
  31.2 2.5 %copy-start = (f32[1,32]{1,0:T(1,128)S(1)}, f32[1,32]{1,0:T(1,128)}, u32[]{:S(2)}) copy-start(f32[1,32]{1,0:T(1,128)} %get-tuple-element.5) | copy-start | bytes 388

commit v3 on v2

--- a/solution.py
+++ b/solution.py
@@ -146,9 +146,9 @@
         pltpu.make_async_copy(src, dst, local_sem.at[i])
         for i, (src, dst) in enumerate(
             [
+                (fields_ref, state.at[:, pl.ds(1, depth)]),
                 (panels_ref, pan_in),
                 (owner_ref, owner_in),
-                (fields_ref, state.at[:, pl.ds(1, depth)]),
                 (solid_ref, solid_in),
                 (cells_ref, cells_in),
                 (geom_ref.at[0, span_pos], geom_in),
@@ -159,18 +159,6 @@
     ]
     for load in loads:
         load.start()
-
-    loads[0].wait()
-    loads[1].wait()
-    owner = jnp.broadcast_to(owner_in[...], (tiles, held))
-    wanted_by = lax.broadcasted_iota(jnp.int32, (tiles, held), 0)
-    route = jnp.where(owner == wanted_by, 1.0, 0.0)
-    for f in range(FIELDS):
-        sums = jnp.dot(
-            route, pan_in[f], precision=HIGHEST, preferred_element_type=jnp.float32
-        )
-        for t in range(tiles):
-            pan_send[t, :, f * spec_cols : (f + 1) * spec_cols] = sums[t : t + 1, :]
 
     def halo(axis, way, src, dst, sem):
         count, place = sizes[axis], me[axis]
@@ -247,8 +235,6 @@
 
     no_columns = tuple(jnp.zeros((span_cells, wind), jnp.float32) for _ in range(groups))
 
-    pl.semaphore_wait(barrier, sum(count - 1 for _, count in meets))
-
     def spread(peers, count, src, dst, mine, send_sem, recv_sem):
         copies = []
         for step in range(1, count):
@@ -273,16 +259,7 @@
             copies.append((copy, arrival))
         return copies
 
-    pan_copies = spread(
-        tile_peer, tiles, lambda peer: pan_send.at[peer], pan_recv, my_tile, pan_s, pan_r
-    )
-    for start, _, _, _ in z_first:
-        start()
-    pan_recv[my_tile] = pan_send[my_tile]
-    for _, _, _, clear in every_halo:
-        clear()
-
-    loads[2].wait()
+    loads[0].wait()
     for part in range(PARTS):
 
         def pack_plane(z, held_x, part=part):
@@ -292,8 +269,28 @@
         packed = lax.fori_loop(0, half, pack_plane, no_columns, unroll=4)
         for g in range(groups):
             x_send[0, part, g] = packed[g]
-    for start, _, _, _ in xy_first:
+    pl.semaphore_wait(barrier, sum(count - 1 for _, count in meets))
+    for start, _, _, _ in z_first + xy_first:
         start()
+    for _, _, _, clear in every_halo:
+        clear()
+
+    loads[1].wait()
+    loads[2].wait()
+    owner = jnp.broadcast_to(owner_in[...], (tiles, held))
+    wanted_by = lax.broadcasted_iota(jnp.int32, (tiles, held), 0)
+    route = jnp.where(owner == wanted_by, 1.0, 0.0)
+    for f in range(FIELDS):
+        sums = jnp.dot(
+            route, pan_in[f], precision=HIGHEST, preferred_element_type=jnp.float32
+        )
+        for t in range(tiles):
+            pan_send[t, :, f * spec_cols : (f + 1) * spec_cols] = sums[t : t + 1, :]
+
+    pan_copies = spread(
+        tile_peer, tiles, lambda peer: pan_send.at[peer], pan_recv, my_tile, pan_s, pan_r
+    )
+    pan_recv[my_tile] = pan_send[my_tile]
 
     total_z, total_y = depth * n_vert, span_cells * n_span
     period = total_y * total_z
@@ -333,47 +330,65 @@
     keep = {nu: 1.0 - time_step * (6.0 * nu) - relax_dt for nu in set(diffusion)}
     half_dt = 0.5 * time_step
 
-    def inflow_term(at):
+    every_field = tuple(range(FIELDS))
+
+    def inflow_term(at, only):
         wanted = target[pl.ds(pl.multiple_of(at * span_cells, span_cells), span_cells), :]
-        return [
-            relax_dt * jnp.broadcast_to(wanted[:, f : f + 1], (span_cells, wind))
-            for f in range(FIELDS)
-        ]
-
-    def advance(source, stage, part, z, inflow=True):
+        return {
+            f: relax_dt * jnp.broadcast_to(wanted[:, f : f + 1], (span_cells, wind))
+            for f in only
+        }
+
+    def advance(source, stage, part, z, inflow=True, only=every_field):
         at = part * half + z
-        terms = inflow_term(at) if inflow else None
+        terms = inflow_term(at, only) if inflow else None
         centre = [source[f, 1 + at] for f in range(FIELDS)]
         u, v, w = (half_dt * centre[f] for f in range(3))
-        diff_x, diff_y, diff_z, new = [], [], [], []
-        for f in range(FIELDS):
-            c = centre[f]
-            pair = (f % per_group) * half + z
-            side = pltpu.roll(x_both[stage, part, f // per_group], wind - 1 - 2 * pair, 1)
-            west = jnp.where(lane == 0, side, pltpu.roll(c, 1, 1))
-            east = jnp.where(lane == wind - 1, side, pltpu.roll(c, wind - 1, 1))
-            low = jnp.broadcast_to(y_recv[stage, 0, part, f, pl.ds(z, 1), :], c.shape)
-            high = jnp.broadcast_to(y_recv[stage, 1, part, f, pl.ds(z, 1), :], c.shape)
-            south = jnp.where(row == 0, low, pltpu.roll(c, 1, 0))
-            north = jnp.where(row == span_cells - 1, high, pltpu.roll(c, span_cells - 1, 0))
-            lower = source[f, at]
-            upper = source[f, at + 2]
-            dx, dy, dz = east - west, north - south, upper - lower
-            around = (east + west) + (north + south) + (upper + lower)
+        sides = {}
+
+        def x_sides(f):
+            if ("x", f) not in sides:
+                c = centre[f]
+                pair = (f % per_group) * half + z
+                side = pltpu.roll(x_both[stage, part, f // per_group], wind - 1 - 2 * pair, 1)
+                west = jnp.where(lane == 0, side, pltpu.roll(c, 1, 1))
+                east = jnp.where(lane == wind - 1, side, pltpu.roll(c, wind - 1, 1))
+                sides["x", f] = east - west, east + west
+            return sides["x", f]
+
+        def y_sides(f):
+            if ("y", f) not in sides:
+                c = centre[f]
+                low = jnp.broadcast_to(y_recv[stage, 0, part, f, pl.ds(z, 1), :], c.shape)
+                high = jnp.broadcast_to(y_recv[stage, 1, part, f, pl.ds(z, 1), :], c.shape)
+                south = jnp.where(row == 0, low, pltpu.roll(c, 1, 0))
+                north = jnp.where(row == span_cells - 1, high, pltpu.roll(c, span_cells - 1, 0))
+                sides["y", f] = north - south, north + south
+            return sides["y", f]
+
+        def z_sides(f):
+            if ("z", f) not in sides:
+                lower, upper = source[f, at], source[f, at + 2]
+                sides["z", f] = upper - lower, upper + lower
+            return sides["z", f]
+
+        damping = (2.0 / penalty) * solid_in[at] if only != (3,) else None
+        new = {}
+        for f in only:
+            (dx, sum_x), (dy, sum_y), (dz, sum_z) = x_sides(f), y_sides(f), z_sides(f)
             nu = diffusion[f]
-            value = keep[nu] * c + (time_step * nu) * around
+            value = keep[nu] * centre[f] + (time_step * nu) * (sum_x + sum_y + sum_z)
             if inflow:
                 value = value + terms[f]
-            value = value - (u * dx + v * dy + w * dz)
-            diff_x.append(dx)
-            diff_y.append(dy)
-            diff_z.append(dz)
-            new.append(value)
-        damping = (2.0 / penalty) * solid_in[at]
-        new[0] = new[0] - half_dt * diff_x[3] - damping * u
-        new[1] = new[1] - half_dt * diff_y[3] - damping * v
-        new[2] = new[2] - half_dt * diff_z[3] - damping * w + (time_step * buoyant) * centre[4]
-        new[3] = new[3] - (half_dt * sound_sq) * (diff_x[0] + diff_y[1] + diff_z[2])
+            new[f] = value - (u * dx + v * dy + w * dz)
+        for f, sided, speed in ((0, x_sides, u), (1, y_sides, v), (2, z_sides, w)):
+            if f in new:
+                new[f] = new[f] - half_dt * sided(3)[0] - damping * speed
+        if 2 in new:
+            new[2] = new[2] + (time_step * buoyant) * centre[4]
+        if 3 in new:
+            spread_out = x_sides(0)[0] + y_sides(1)[0] + z_sides(2)[0]
+            new[3] = new[3] - (half_dt * sound_sq) * spread_out
         return new
 
     loads[3].wait()
@@ -419,7 +434,7 @@
     target[...] = inflow + jnp.where(first_field, 1.0, 0.0)
 
     def finish_plane(z, held_x):
-        terms = inflow_term(z)
+        terms = inflow_term(z, every_field)
         new = [update[f, 1 + z] + terms[f] for f in range(FIELDS)]
         for f in range(FIELDS):
             update[f, 1 + z] = new[f]
@@ -439,10 +454,10 @@
             start()
         z_second[1 - part][0]()
 
-    def second_plane(part, z):
-        new = advance(update, 1, part, z)
+    def second_plane(part, z, only=every_field):
+        new = advance(update, 1, part, z, only=only)
         at = part * half + z
-        for f in range(FIELDS):
+        for f in only:
             value = 0.5 * (state[f, 1 + at] + new[f])
             result[f, at] = value
             if f == 3:
@@ -466,7 +481,7 @@
             z_second[1][1]()
 
         def plane_step(z, carry, part=part):
-            second_plane(part, z)
+            second_plane(part, z, every_field if part == 0 else (3,))
             return carry
 
         if part == 0:
@@ -474,9 +489,9 @@
             z_second[0][1]()
             second_plane(0, 0)
             second_plane(0, 1)
+            store(0).start()
         else:
-            lax.fori_loop(0, half, plane_step, 0, unroll=2)
-        store(part).start()
+            lax.fori_loop(0, half, plane_step, 0, unroll=4)
 
     for load in loads[4:]:
         load.wait()
@@ -511,6 +526,11 @@
         [modes_in[n % 3, pl.ds(base + n // 3, 1), :] for n in range(3 * strip_share)], axis=0
     )
     part_force = jnp.sum(force * shapes, axis=0, keepdims=True)
+
+    def other_fields(z, carry):
+        second_plane(1, z, (0, 1, 2, 4))
+        return carry
+
     md_copies = []
     slots = ((md_recv, md_s, md_r), (sd_recv, sd_s, sd_r))
     for hop, (peers, count, mine) in enumerate(hops):
@@ -522,6 +542,8 @@
         )
         recv[mine] = md_send[hop]
         if hop == 0:
+            lax.fori_loop(0, half, other_fields, 0, unroll=2)
+            store(1).start()
             for copy, _ in pan_copies + co_copies:
                 copy.wait_send()
             for _, _, leave, _ in every_halo:
@@ -538,6 +560,25 @@
     modal_ref[...] = part_force
     for copy, _ in md_copies:
         copy.wait_send()
+
+
+def place(fields_ref, modal_ref, out_ref, force_ref, held, force, in_sem, out_sem):
+    count = fields_ref.shape[0]
+    pieces = [(modal_ref, force, force_ref)]
+    pieces += [(fields_ref.at[f], held.at[f], out_ref.at[f]) for f in range(count)]
+    comes = [
+        pltpu.make_async_copy(src, mid, in_sem.at[i]) for i, (src, mid, _) in enumerate(pieces)
+    ]
+    goes = [
+        pltpu.make_async_copy(mid, dst, out_sem.at[i]) for i, (_, mid, dst) in enumerate(pieces)
+    ]
+    for come in comes:
+        come.start()
+    for come, go in zip(comes, goes):
+        come.wait()
+        go.start()
+    for go in goes:
+        go.wait()
 
 
 def on_device(sizes, fields, solid, panels, owner, cells, geom, strips, modes):
@@ -614,6 +655,23 @@
         ),
         name="wind_steps",
     )(fields, solid, panels, owner, cells, geom, strips, modes)
+    new_fields, modal = pl.pallas_call(
+        place,
+        out_shape=(
+            jax.ShapeDtypeStruct(fields.shape, f32),
+            jax.ShapeDtypeStruct((1, n_modes), f32),
+        ),
+        in_specs=[hbm, hbm],
+        out_specs=(hbm, hbm),
+        scratch_shapes=[
+            pltpu.VMEM(fields.shape, f32),
+            pltpu.VMEM((1, n_modes), f32),
+            dma((FIELDS + 1,)),
+            dma((FIELDS + 1,)),
+        ],
+        compiler_params=pltpu.CompilerParams(vmem_limit_bytes=63 * 1024 * 1024),
+        name="place_results",
+    )(new_fields, modal)
     return new_fields, modal[0]
 
 

time: 34.4 us -> 33 us (0.959)
  local copies, waits for them, and re-layouts: 3.02 us -> 0 us
  Pallas kernels: 30.6 us -> 32.2 us
    unnamed x4 -> x0, local copies, waits for them, and re-layouts: 3.02 us -> none
    pallas_call x0 -> x1, Pallas kernels: none -> 2.11 us  [on_device(): pl.pallas_call(place, out_shape=(jax.ShapeDtypeStruct(fields.shape, f32),...]
    pallas_call x1, Pallas kernels: 30.6 us -> 30.1 us  [on_device(): pl.pallas_call(functools.partial(kernel, sizes), out_shape=(jax.ShapeDtyp...]
where the time goes in v3:
time: 33 us; the launch traced here: 32.9 us
  Pallas kernels  32.2 us (98%)
  between operations  0.64 us (2%)
    pallas_call x1, Pallas kernels, on_device(): pl.pallas_call(functools.partial(kernel, sizes), out_shape=(jax.ShapeDtyp...  30.1 us
    pallas_call x1, Pallas kernels, on_device(): pl.pallas_call(place, out_shape=(jax.ShapeDtypeStruct(fields.shape, f32),...  2.11 us

profile of v3, /device:TPU:0, one launch (start us, length us, event | category | flops | bytes accessed | tf_op | source)
XLA Modules:
  0.0 32.9 jit_solution(15243885219393917050)
XLA Ops:
  0.6 30.1 %wind_steps.1 = (f32[5,32,16,128]{3,2,1,0:T(8,128)}, f32[1,32]{1,0:T(1,128)}) custom-call(f32[5,32,16,128]{3,2,1,0:T(8,128)} %fields_ref.1, f32[32,16,128]{2,1,0:T(8,128)} %solid_ref.1, f32[5,16,256]{2,1,0:T(8,128)} %bitcast.5, s32[1,16]{1,0:T(1,128)} %bitcast.6, s32[1,1,1,2048]{3,2,1,0:T(1,128)} %cells_ref.1, f32[1,4,3,1,2048]{4,3,2,1,0:T(1,128)} %bitcast.4, ...), custom_call_target="tpu_custom_call" | custom-call | tf_op jit(solution)/shard_map/wind_steps/pallas_call | solution.py:606
  30.8 2.1 %place_results.1 = (f32[5,32,16,128]{3,2,1,0:T(8,128)}, f32[1,32]{1,0:T(1,128)}) custom-call(f32[5,32,16,128]{3,2,1,0:T(8,128)} %get-tuple-element.6.fields_ref, f32[1,32]{1,0:T(1,128)} %get-tuple-element.7.modal_ref), custom_call_target="tpu_custom_call" | custom-call | tf_op jit(solution)/shard_map/place_results/pallas_call | solution.py:658

commit v4 on v3

--- a/solution.py
+++ b/solution.py
@@ -160,6 +160,22 @@
     for load in loads:
         load.start()
 
+    total_z, total_y = depth * n_vert, span_cells * n_span
+    period = total_y * total_z
+    plane = depth * span_cells
+    cell_z, cell_y = split_index(lax.broadcasted_iota(jnp.int32, (plane, spec), 0), span_cells)
+    upward, across = split_index(lax.broadcasted_iota(jnp.int32, (plane, spec), 1), wave_cols)
+    phase = across * (span_pos * span_cells + cell_y) * total_z
+    phase = phase + upward * (vert_pos * depth + cell_z) * total_y
+    phase = split_index(phase, period)[1]
+    cosine, sine = circle(phase.astype(jnp.float32) * (1.0 / period))
+    for i, values in enumerate((cosine, sine)):
+        top = values.astype(jnp.bfloat16)
+        rest = (values - top.astype(jnp.float32)).astype(jnp.bfloat16)
+        wave[:, i * spec : (i + 1) * spec] = top
+        wave[:, spec_cols + i * spec : spec_cols + (i + 1) * spec] = top
+        wave[:, 2 * spec_cols + i * spec : 2 * spec_cols + (i + 1) * spec] = rest
+
     def halo(axis, way, src, dst, sem):
         count, place = sizes[axis], me[axis]
         up = way == 0
@@ -202,21 +218,33 @@
         halo(2, 0, update.at[:, depth], update.at[:, 0], 2),
         halo(2, 1, update.at[:, 1], update.at[:, depth + 1], 3),
     ]
-    xy_first = [
-        halo(1, way, y_send.at[0, way], y_recv.at[0, way], 4 + way) for way in range(2)
-    ] + [halo(0, way, x_send.at[0], x_recv.at[0, way], 6 + way) for way in range(2)]
-    xy_second = [
+    xy_first, xy_second = (
         [
-            halo(1, way, y_send.at[1, way, part], y_recv.at[1, way, part], 8 + 4 * part + way)
-            for way in range(2)
+            [
+                halo(
+                    1,
+                    way,
+                    y_send.at[stage, way, part],
+                    y_recv.at[stage, way, part],
+                    4 + 8 * stage + 4 * part + way,
+                )
+                for way in range(2)
+            ]
+            + [
+                halo(
+                    0,
+                    way,
+                    x_send.at[stage, part],
+                    x_recv.at[stage, way, part],
+                    6 + 8 * stage + 4 * part + way,
+                )
+                for way in range(2)
+            ]
+            for part in range(PARTS)
         ]
-        + [
-            halo(0, way, x_send.at[1, part], x_recv.at[1, way, part], 10 + 4 * part + way)
-            for way in range(2)
-        ]
-        for part in range(PARTS)
-    ]
-    every_halo = z_first + z_second + xy_first + xy_second[0] + xy_second[1]
+        for stage in range(2)
+    )
+    every_halo = z_first + z_second + sum(xy_first + xy_second, [])
 
     lane = lax.broadcasted_iota(jnp.int32, (span_cells, wind), 1)
     row = lax.broadcasted_iota(jnp.int32, (span_cells, wind), 0)
@@ -269,9 +297,10 @@
         packed = lax.fori_loop(0, half, pack_plane, no_columns, unroll=4)
         for g in range(groups):
             x_send[0, part, g] = packed[g]
-    pl.semaphore_wait(barrier, sum(count - 1 for _, count in meets))
-    for start, _, _, _ in z_first + xy_first:
-        start()
+        if part == 0:
+            pl.semaphore_wait(barrier, sum(count - 1 for _, count in meets))
+        for start, _, _, _ in xy_first[part] + [z_first[part]]:
+            start()
     for _, _, _, clear in every_halo:
         clear()
 
@@ -292,24 +321,6 @@
     )
     pan_recv[my_tile] = pan_send[my_tile]
 
-    total_z, total_y = depth * n_vert, span_cells * n_span
-    period = total_y * total_z
-    plane = depth * span_cells
-    cell_z, cell_y = split_index(lax.broadcasted_iota(jnp.int32, (plane, spec), 0), span_cells)
-    upward, across = split_index(lax.broadcasted_iota(jnp.int32, (plane, spec), 1), wave_cols)
-    phase = across * (span_pos * span_cells + cell_y) * total_z
-    phase = phase + upward * (vert_pos * depth + cell_z) * total_y
-    phase = split_index(phase, period)[1]
-    cosine, sine = circle(phase.astype(jnp.float32) * (1.0 / period))
-    for i, values in enumerate((cosine, sine)):
-        top = values.astype(jnp.bfloat16)
-        rest = (values - top.astype(jnp.float32)).astype(jnp.bfloat16)
-        wave[:, i * spec : (i + 1) * spec] = top
-        wave[:, spec_cols + i * spec : spec_cols + (i + 1) * spec] = top
-        wave[:, 2 * spec_cols + i * spec : 2 * spec_cols + (i + 1) * spec] = rest
-
-    for _, arrive, _, _ in z_first + xy_first:
-        arrive()
     even = (lane & 1) == 0
 
     def columns(stage, part):
@@ -317,9 +328,6 @@
             from_low = pltpu.roll(x_recv[stage, 0, part, g], 1, 1)
             from_high = pltpu.roll(x_recv[stage, 1, part, g], wind - 1, 1)
             x_both[stage, part, g] = jnp.where(even, from_high, from_low)
-
-    for part in range(PARTS):
-        columns(0, part)
 
     spots = stream_pos * wind + lane
     relax = jnp.where(
@@ -392,6 +400,9 @@
         return new
 
     loads[3].wait()
+    for _, arrive, _, _ in xy_first[0] + [z_first[0]]:
+        arrive()
+    columns(0, 0)
 
     def plain_plane(z, carry):
         new = advance(state, 0, 0, z, inflow=False)
@@ -399,7 +410,7 @@
             update[f, 1 + z] = new[f]
         return carry
 
-    lax.fori_loop(0, half // 2, plain_plane, 0, unroll=2)
+    lax.fori_loop(0, half // 2, plain_plane, 0, unroll=4)
 
     for _, arrival in pan_copies:
         arrival.wait_recv()
@@ -412,7 +423,7 @@
     )
     co_recv[stream_pos] = mine
 
-    lax.fori_loop(half // 2, half, plain_plane, 0, unroll=2)
+    lax.fori_loop(half // 2, half, plain_plane, 0, unroll=4)
 
     for _, arrival in co_copies:
         arrival.wait_recv()
@@ -446,8 +457,12 @@
             update[f, 1 + half + z] = new[f]
         return pack(1, 1, z, new, held_x)
 
-    for part, (step_plane, turns) in enumerate(((finish_plane, 4), (first_plane, 2))):
-        packed = lax.fori_loop(0, half, step_plane, no_columns, unroll=turns)
+    for part, step_plane in enumerate((finish_plane, first_plane)):
+        if part == 1:
+            for _, arrive, _, _ in xy_first[1] + [z_first[1]]:
+                arrive()
+            columns(0, 1)
+        packed = lax.fori_loop(0, half, step_plane, no_columns, unroll=4)
         for g in range(groups):
             x_send[1, part, g] = packed[g]
         for start, _, _, _ in xy_second[part]:
@@ -485,10 +500,9 @@
             return carry
 
         if part == 0:
-            lax.fori_loop(2, half, plane_step, 0, unroll=2)
+            lax.fori_loop(half // 4, half, plane_step, 0, unroll=4)
             z_second[0][1]()
-            second_plane(0, 0)
-            second_plane(0, 1)
+            lax.fori_loop(0, half // 4, plane_step, 0, unroll=4)
             store(0).start()
         else:
             lax.fori_loop(0, half, plane_step, 0, unroll=4)
@@ -542,7 +556,7 @@
         )
         recv[mine] = md_send[hop]
         if hop == 0:
-            lax.fori_loop(0, half, other_fields, 0, unroll=2)
+            lax.fori_loop(0, half, other_fields, 0, unroll=4)
             store(1).start()
             for copy, _ in pan_copies + co_copies:
                 copy.wait_send()
@@ -562,23 +576,17 @@
         copy.wait_send()
 
 
-def place(fields_ref, modal_ref, out_ref, force_ref, held, force, in_sem, out_sem):
+def place(fields_ref, modal_ref, out_ref, force_ref, sem):
     count = fields_ref.shape[0]
-    pieces = [(modal_ref, force, force_ref)]
-    pieces += [(fields_ref.at[f], held.at[f], out_ref.at[f]) for f in range(count)]
-    comes = [
-        pltpu.make_async_copy(src, mid, in_sem.at[i]) for i, (src, mid, _) in enumerate(pieces)
+    pieces = [(modal_ref, force_ref)]
+    pieces += [(fields_ref.at[f], out_ref.at[f]) for f in range(count)]
+    copies = [
+        pltpu.make_async_copy(src, dst, sem.at[i]) for i, (src, dst) in enumerate(pieces)
     ]
-    goes = [
-        pltpu.make_async_copy(mid, dst, out_sem.at[i]) for i, (_, mid, dst) in enumerate(pieces)
-    ]
-    for come in comes:
-        come.start()
-    for come, go in zip(comes, goes):
-        come.wait()
-        go.start()
-    for go in goes:
-        go.wait()
+    for copy in copies:
+        copy.start()
+    for copy in copies:
+        copy.wait()
 
 
 def on_device(sizes, fields, solid, panels, owner, cells, geom, strips, modes):
@@ -639,8 +647,8 @@
             pltpu.VMEM((first_hop, 1, 128), f32),
             pltpu.VMEM((second_hop, 1, 128), f32),
             dma((8 + PARTS,)),
-            dma((8 + 4 * PARTS,)),
-            dma((8 + 4 * PARTS,)),
+            dma((4 + 8 * PARTS,)),
+            dma((4 + 8 * PARTS,)),
             dma((tiles,)),
             dma((tiles,)),
             dma((n_stream,)),
@@ -664,9 +672,6 @@
         in_specs=[hbm, hbm],
         out_specs=(hbm, hbm),
         scratch_shapes=[
-            pltpu.VMEM(fields.shape, f32),
-            pltpu.VMEM((1, n_modes), f32),
-            dma((FIELDS + 1,)),
             dma((FIELDS + 1,)),
         ],
         compiler_params=pltpu.CompilerParams(vmem_limit_bytes=63 * 1024 * 1024),

time: 33 us -> 71.9 us (2.18)
  Pallas kernels: 32.2 us -> 71.1 us
    pallas_call x1, Pallas kernels: 2.11 us -> 40.9 us  [on_device(): pl.pallas_call(place, out_shape=(jax.ShapeDtypeStruct(fields.shape, f32),...]
where the time goes in v4:
time: 71.9 us; the launch traced here: 71.7 us
  Pallas kernels  71.1 us (99%)
    pallas_call x1, Pallas kernels, on_device(): pl.pallas_call(place, out_shape=(jax.ShapeDtypeStruct(fields.shape, f32),...  40.9 us
    pallas_call x1, Pallas kernels, on_device(): pl.pallas_call(functools.partial(kernel, sizes), out_shape=(jax.ShapeDtyp...  30.2 us

profile of v4, /device:TPU:0, one launch (start us, length us, event | category | flops | bytes accessed | tf_op | source)
XLA Modules:
  0.0 71.7 jit_solution(1872577117302375641)
XLA Ops:
  0.6 30.2 %wind_steps.1 = (f32[5,32,16,128]{3,2,1,0:T(8,128)}, f32[1,32]{1,0:T(1,128)}) custom-call(f32[5,32,16,128]{3,2,1,0:T(8,128)} %fields_ref.1, f32[32,16,128]{2,1,0:T(8,128)} %solid_ref.1, f32[5,16,256]{2,1,0:T(8,128)} %bitcast.5, s32[1,16]{1,0:T(1,128)} %bitcast.6, s32[1,1,1,2048]{3,2,1,0:T(1,128)} %cells_ref.1, f32[1,4,3,1,2048]{4,3,2,1,0:T(1,128)} %bitcast.4, ...), custom_call_target="tpu_custom_call" | custom-call | tf_op jit(solution)/shard_map/wind_steps/pallas_call | solution.py:614
  30.9 40.9 %place_results.1 = (f32[5,32,16,128]{3,2,1,0:T(8,128)}, f32[1,32]{1,0:T(1,128)}) custom-call(f32[5,32,16,128]{3,2,1,0:T(8,128)} %get-tuple-element.6.fields_ref, f32[1,32]{1,0:T(1,128)} %get-tuple-element.7.modal_ref), custom_call_target="tpu_custom_call" | custom-call | tf_op jit(solution)/shard_map/place_results/pallas_call | solution.py:666

commit v5 on v4

--- a/solution.py
+++ b/solution.py
@@ -1,4 +1,5 @@
 import functools
+import itertools
 import math
 
 import jax
@@ -114,33 +115,33 @@
     stream_pos, span_pos, vert_pos = me
     my_tile = span_pos * n_vert + vert_pos
 
-    def tile_peer(step):
-        peer = lax.rem(my_tile + step, tiles)
-        whole = lax.div(peer, jnp.int32(n_vert))
-        return peer, (stream_pos, whole, peer - whole * n_vert)
-
-    def stream_peer(step):
-        peer = lax.rem(stream_pos + step, n_stream)
-        return peer, (peer, span_pos, vert_pos)
-
-    def any_peer(step):
-        peer = lax.rem(stream_pos * tiles + my_tile + step, n_stream * tiles)
-        stream = lax.div(peer, jnp.int32(tiles))
-        rest = peer - stream * tiles
-        whole = lax.div(rest, jnp.int32(n_vert))
-        return peer, (stream, whole, rest - whole * n_vert)
-
-    one_hop = n_stream * tiles <= ONE_HOP
-    if one_hop:
-        meets = [(any_peer, n_stream * tiles)]
-        hops = [(any_peer, n_stream * tiles, stream_pos * tiles + my_tile)]
+    def wrapped(place, offset, count):
+        moved = place + offset
+        return jnp.where(moved >= count, moved - count, moved)
+
+    def peers_over(axes):
+        found = []
+        for offsets in itertools.product(*(range(sizes[a]) for a in axes)):
+            if any(offsets):
+                device, slot = list(me), 0
+                for a, offset in zip(axes, offsets):
+                    device[a] = wrapped(me[a], offset, sizes[a]) if offset else me[a]
+                    slot = slot * sizes[a] + device[a]
+                found.append((slot, tuple(device)))
+        return found
+
+    tile_peers = peers_over((1, 2))
+    stream_peers = peers_over((0,))
+    if n_stream * tiles <= ONE_HOP:
+        all_peers = peers_over((0, 1, 2))
+        meets = all_peers
+        hops = [(all_peers, stream_pos * tiles + my_tile)]
     else:
-        meets = [(tile_peer, tiles), (stream_peer, n_stream)]
-        hops = [(tile_peer, tiles, my_tile), (stream_peer, n_stream, stream_pos)]
+        meets = tile_peers + stream_peers
+        hops = [(tile_peers, my_tile), (stream_peers, stream_pos)]
     barrier = pltpu.get_barrier_semaphore()
-    for peers, count in meets:
-        for step in range(1, count):
-            pl.semaphore_signal(barrier, inc=1, device_id=peers(step)[1], device_id_type=MESH)
+    for _, device in meets:
+        pl.semaphore_signal(barrier, inc=1, device_id=device, device_id_type=MESH)
 
     loads = [
         pltpu.make_async_copy(src, dst, local_sem.at[i])
@@ -179,7 +180,7 @@
     def halo(axis, way, src, dst, sem):
         count, place = sizes[axis], me[axis]
         up = way == 0
-        to = lax.rem(place + (1 if up else count - 1), count)
+        to = wrapped(place, 1 if up else count - 1, count)
         device = tuple(to if a == axis else me[a] for a in range(3))
         sends = place < count - 1 if up else place > 0
         gets = place > 0 if up else place < count - 1
@@ -211,8 +212,8 @@
         return start, arrive, leave, clear
 
     z_first = [
-        halo(2, 0, fields_ref.at[:, depth - 1], state.at[:, 0], 0),
-        halo(2, 1, fields_ref.at[:, 0], state.at[:, depth + 1], 1),
+        halo(2, 0, state.at[:, depth], state.at[:, 0], 0),
+        halo(2, 1, state.at[:, 1], state.at[:, depth + 1], 1),
     ]
     z_second = [
         halo(2, 0, update.at[:, depth], update.at[:, 0], 2),
@@ -263,29 +264,25 @@
 
     no_columns = tuple(jnp.zeros((span_cells, wind), jnp.float32) for _ in range(groups))
 
-    def spread(peers, count, src, dst, mine, send_sem, recv_sem):
-        copies = []
-        for step in range(1, count):
-            peer, device = peers(step)
-            copy = pltpu.make_async_remote_copy(
-                src_ref=src(peer),
+    def spread(peers, src, dst, mine, send_sem, recv_sem):
+        for slot, device in peers:
+            pltpu.make_async_remote_copy(
+                src_ref=src(slot),
                 dst_ref=dst.at[mine],
-                send_sem=send_sem.at[peer],
-                recv_sem=recv_sem.at[mine],
+                send_sem=send_sem.at[0],
+                recv_sem=recv_sem.at[0],
                 device_id=device,
                 device_id_type=MESH,
-            )
-            copy.start()
-            arrival = pltpu.make_async_remote_copy(
-                src_ref=src(peer),
-                dst_ref=dst.at[peer],
-                send_sem=send_sem.at[peer],
-                recv_sem=recv_sem.at[peer],
-                device_id=device,
-                device_id_type=MESH,
-            )
-            copies.append((copy, arrival))
-        return copies
+            ).start()
+        others = dst.at[pl.ds(0, len(peers))]
+
+        def arrive():
+            pltpu.make_async_copy(others, others, recv_sem.at[0]).wait()
+
+        def leave():
+            pltpu.make_async_copy(others, others, send_sem.at[0]).wait()
+
+        return arrive, leave
 
     loads[0].wait()
     for part in range(PARTS):
@@ -298,7 +295,7 @@
         for g in range(groups):
             x_send[0, part, g] = packed[g]
         if part == 0:
-            pl.semaphore_wait(barrier, sum(count - 1 for _, count in meets))
+            pl.semaphore_wait(barrier, len(meets))
         for start, _, _, _ in xy_first[part] + [z_first[part]]:
             start()
     for _, _, _, clear in every_halo:
@@ -316,8 +313,8 @@
         for t in range(tiles):
             pan_send[t, :, f * spec_cols : (f + 1) * spec_cols] = sums[t : t + 1, :]
 
-    pan_copies = spread(
-        tile_peer, tiles, lambda peer: pan_send.at[peer], pan_recv, my_tile, pan_s, pan_r
+    pan_arrive, pan_leave = spread(
+        tile_peers, lambda slot: pan_send.at[slot], pan_recv, my_tile, pan_s, pan_r
     )
     pan_recv[my_tile] = pan_send[my_tile]
 
@@ -412,21 +409,19 @@
 
     lax.fori_loop(0, half // 2, plain_plane, 0, unroll=4)
 
-    for _, arrival in pan_copies:
-        arrival.wait_recv()
+    pan_arrive()
     mine = pan_recv[0]
     for t in range(1, tiles):
         mine = mine + pan_recv[t]
     co_send[...] = mine
-    co_copies = spread(
-        stream_peer, n_stream, lambda peer: co_send, co_recv, stream_pos, co_s, co_r
+    co_arrive, co_leave = spread(
+        stream_peers, lambda slot: co_send, co_recv, stream_pos, co_s, co_r
     )
     co_recv[stream_pos] = mine
 
     lax.fori_loop(half // 2, half, plain_plane, 0, unroll=4)
 
-    for _, arrival in co_copies:
-        arrival.wait_recv()
+    co_arrive()
     coeffs = co_recv[0]
     for t in range(1, n_stream):
         coeffs = coeffs + co_recv[t]
@@ -545,48 +540,49 @@
         second_plane(1, z, (0, 1, 2, 4))
         return carry
 
-    md_copies = []
+    leaves = [pan_leave, co_leave] + [leave for _, _, leave, _ in every_halo]
     slots = ((md_recv, md_s, md_r), (sd_recv, sd_s, sd_r))
-    for hop, (peers, count, mine) in enumerate(hops):
+    for hop, (peers, mine) in enumerate(hops):
         recv, send_sem, recv_sem = slots[hop]
         md_send[hop] = jnp.zeros(md_send.shape[1:], jnp.float32)
         md_send[hop, :, 0:n_modes] = part_force
-        copies = spread(
-            peers, count, lambda peer, hop=hop: md_send.at[hop], recv, mine, send_sem, recv_sem
+        arrive, leave = spread(
+            peers, lambda slot, hop=hop: md_send.at[hop], recv, mine, send_sem, recv_sem
         )
         recv[mine] = md_send[hop]
         if hop == 0:
             lax.fori_loop(0, half, other_fields, 0, unroll=4)
             store(1).start()
-            for copy, _ in pan_copies + co_copies:
-                copy.wait_send()
-            for _, _, leave, _ in every_halo:
-                leave()
+            for done in leaves:
+                done()
             for part in range(PARTS):
                 store(part).wait()
-        for _, arrival in copies:
-            arrival.wait_recv()
+        arrive()
         total = recv[0]
-        for t in range(1, count):
+        for t in range(1, len(peers) + 1):
             total = total + recv[t]
         part_force = total[:, 0:n_modes]
-        md_copies = md_copies + copies
+        leave()
     modal_ref[...] = part_force
-    for copy, _ in md_copies:
-        copy.wait_send()
-
-
-def place(fields_ref, modal_ref, out_ref, force_ref, sem):
+
+
+def place(fields_ref, modal_ref, out_ref, force_ref, held, force, in_sem, out_sem):
     count = fields_ref.shape[0]
-    pieces = [(modal_ref, force_ref)]
-    pieces += [(fields_ref.at[f], out_ref.at[f]) for f in range(count)]
-    copies = [
-        pltpu.make_async_copy(src, dst, sem.at[i]) for i, (src, dst) in enumerate(pieces)
+    pieces = [(fields_ref.at[f], held.at[f], out_ref.at[f]) for f in range(count)]
+    pieces += [(modal_ref, force, force_ref)]
+    comes = [
+        pltpu.make_async_copy(src, mid, in_sem.at[i]) for i, (src, mid, _) in enumerate(pieces)
     ]
-    for copy in copies:
-        copy.start()
-    for copy in copies:
-        copy.wait()
+    goes = [
+        pltpu.make_async_copy(mid, dst, out_sem.at[i]) for i, (_, mid, dst) in enumerate(pieces)
+    ]
+    for come in comes:
+        come.start()
+    for come, go in zip(comes, goes):
+        come.wait()
+        go.start()
+    for go in goes:
+        go.wait()
 
 
 def on_device(sizes, fields, solid, panels, owner, cells, geom, strips, modes):
@@ -649,14 +645,14 @@
             dma((8 + PARTS,)),
             dma((4 + 8 * PARTS,)),
             dma((4 + 8 * PARTS,)),
-            dma((tiles,)),
-            dma((tiles,)),
-            dma((n_stream,)),
-            dma((n_stream,)),
-            dma((first_hop,)),
-            dma((first_hop,)),
-            dma((second_hop,)),
-            dma((second_hop,)),
+            dma((1,)),
+            dma((1,)),
+            dma((1,)),
+            dma((1,)),
+            dma((1,)),
+            dma((1,)),
+            dma((1,)),
+            dma((1,)),
         ],
         compiler_params=pltpu.CompilerParams(
             collective_id=0, has_side_effects=True, vmem_limit_bytes=63 * 1024 * 1024
@@ -672,6 +668,9 @@
         in_specs=[hbm, hbm],
         out_specs=(hbm, hbm),
         scratch_shapes=[
+            pltpu.VMEM(fields.shape, f32),
+            pltpu.VMEM((1, n_modes), f32),
+            dma((FIELDS + 1,)),
             dma((FIELDS + 1,)),
         ],
         compiler_params=pltpu.CompilerParams(vmem_limit_bytes=63 * 1024 * 1024),

time: 71.9 us -> 32.5 us (0.45)
  Pallas kernels: 71.1 us -> 31.7 us
    pallas_call x1, Pallas kernels: 40.9 us -> 2.1 us  [on_device(): pl.pallas_call(place, out_shape=(jax.ShapeDtypeStruct(fields.shape, f32),...]
where the time goes in v5:
time: 32.5 us; the launch traced here: 32.3 us
  Pallas kernels  31.7 us (98%)
  between operations  0.64 us (2%)
    pallas_call x1, Pallas kernels, on_device(): pl.pallas_call(functools.partial(kernel, sizes), out_shape=(jax.ShapeDtyp...  29.5 us
    pallas_call x1, Pallas kernels, on_device(): pl.pallas_call(place, out_shape=(jax.ShapeDtypeStruct(fields.shape, f32),...  2.1 us

profile of v5, /device:TPU:0, one launch (start us, length us, event | category | flops | bytes accessed | tf_op | source)
XLA Modules:
  0.0 32.3 jit_solution(807487167121323434)
XLA Ops:
  0.6 29.5 %wind_steps.1 = (f32[5,32,16,128]{3,2,1,0:T(8,128)}, f32[1,32]{1,0:T(1,128)}) custom-call(f32[5,32,16,128]{3,2,1,0:T(8,128)} %fields_ref.1, f32[32,16,128]{2,1,0:T(8,128)} %solid_ref.1, f32[5,16,256]{2,1,0:T(8,128)} %bitcast.5, s32[1,16]{1,0:T(1,128)} %bitcast.6, s32[1,1,1,2048]{3,2,1,0:T(1,128)} %cells_ref.1, f32[1,4,3,1,2048]{4,3,2,1,0:T(1,128)} %bitcast.4, ...), custom_call_target="tpu_custom_call" | custom-call | tf_op jit(solution)/shard_map/wind_steps/pallas_call | solution.py:610
  30.2 2.1 %place_results.1 = (f32[5,32,16,128]{3,2,1,0:T(8,128)}, f32[1,32]{1,0:T(1,128)}) custom-call(f32[5,32,16,128]{3,2,1,0:T(8,128)} %get-tuple-element.6.fields_ref, f32[1,32]{1,0:T(1,128)} %get-tuple-element.7.modal_ref), custom_call_target="tpu_custom_call" | custom-call | tf_op jit(solution)/shard_map/place_results/pallas_call | solution.py:662

commit v6 on v5

--- a/solution.py
+++ b/solution.py
@@ -83,6 +83,7 @@
     co_rows,
     wave,
     target,
+    nudge,
     press,
     md_send,
     md_recv,
@@ -339,14 +340,18 @@
 
     def inflow_term(at, only):
         wanted = target[pl.ds(pl.multiple_of(at * span_cells, span_cells), span_cells), :]
-        return {
+        terms = {
             f: relax_dt * jnp.broadcast_to(wanted[:, f : f + 1], (span_cells, wind))
             for f in only
         }
+        for f in only:
+            nudge[f, at] = terms[f]
+        return terms
 
     def advance(source, stage, part, z, inflow=True, only=every_field):
         at = part * half + z
-        terms = inflow_term(at, only) if inflow else None
+        if inflow:
+            terms = inflow_term(at, only) if stage == 0 else {f: nudge[f, at] for f in only}
         centre = [source[f, 1 + at] for f in range(FIELDS)]
         u, v, w = (half_dt * centre[f] for f in range(3))
         sides = {}
@@ -638,6 +643,7 @@
             pltpu.VMEM((16, spec_cols), f32),
             pltpu.VMEM((plane, 3 * spec_cols), jnp.bfloat16),
             pltpu.VMEM((plane, 16), f32),
+            pltpu.VMEM((FIELDS, depth, span_cells, wind), f32),
             pltpu.VMEM((plane, 2 * wind), jnp.bfloat16),
             pltpu.VMEM((2, 1, 128), f32),
             pltpu.VMEM((first_hop, 1, 128), f32),

time: 32.5 us -> 32.4 us (level)
  no operation moved by 1% of the time
where the time goes in v6:
time: 32.4 us; the launch traced here: 32.3 us
  Pallas kernels  31.6 us (98%)
  between operations  0.64 us (2%)
    pallas_call x1, Pallas kernels, on_device(): pl.pallas_call(functools.partial(kernel, sizes), out_shape=(jax.ShapeDtyp...  29.5 us
    pallas_call x1, Pallas kernels, on_device(): pl.pallas_call(place, out_shape=(jax.ShapeDtypeStruct(fields.shape, f32),...  2.1 us

profile of v6, /device:TPU:0, one launch (start us, length us, event | category | flops | bytes accessed | tf_op | source)
XLA Modules:
  0.0 32.3 jit_solution(15310013960446935381)
XLA Ops:
  0.6 29.5 %wind_steps.1 = (f32[5,32,16,128]{3,2,1,0:T(8,128)}, f32[1,32]{1,0:T(1,128)}) custom-call(f32[5,32,16,128]{3,2,1,0:T(8,128)} %fields_ref.1, f32[32,16,128]{2,1,0:T(8,128)} %solid_ref.1, f32[5,16,256]{2,1,0:T(8,128)} %bitcast.5, s32[1,16]{1,0:T(1,128)} %bitcast.6, s32[1,1,1,2048]{3,2,1,0:T(1,128)} %cells_ref.1, f32[1,4,3,1,2048]{4,3,2,1,0:T(1,128)} %bitcast.4, ...), custom_call_target="tpu_custom_call" | custom-call | tf_op jit(solution)/shard_map/wind_steps/pallas_call | solution.py:615
  30.2 2.1 %place_results.1 = (f32[5,32,16,128]{3,2,1,0:T(8,128)}, f32[1,32]{1,0:T(1,128)}) custom-call(f32[5,32,16,128]{3,2,1,0:T(8,128)} %get-tuple-element.6.fields_ref, f32[1,32]{1,0:T(1,128)} %get-tuple-element.7.modal_ref), custom_call_target="tpu_custom_call" | custom-call | tf_op jit(solution)/shard_map/place_results/pallas_call | solution.py:668

commit v7 on v6

--- a/solution.py
+++ b/solution.py
@@ -483,7 +483,7 @@
                 press[where, wind:] = rest
 
     def store(part):
-        where = pl.ds(part * half, half)
+        where = pl.ds(part * (half // 2), half // 2)
         return pltpu.make_async_copy(
             result.at[:, where], out_ref.at[:, where], local_sem.at[8 + part]
         )
@@ -504,6 +504,7 @@
             z_second[0][1]()
             lax.fori_loop(0, half // 4, plane_step, 0, unroll=4)
             store(0).start()
+            store(1).start()
         else:
             lax.fori_loop(0, half, plane_step, 0, unroll=4)
 
@@ -556,11 +557,13 @@
         )
         recv[mine] = md_send[hop]
         if hop == 0:
-            lax.fori_loop(0, half, other_fields, 0, unroll=4)
-            store(1).start()
+            lax.fori_loop(0, half // 2, other_fields, 0, unroll=4)
+            store(2).start()
+            lax.fori_loop(half // 2, half, other_fields, 0, unroll=4)
+            store(3).start()
             for done in leaves:
                 done()
-            for part in range(PARTS):
+            for part in range(2 * PARTS):
                 store(part).wait()
         arrive()
         total = recv[0]
@@ -573,7 +576,9 @@
 
 def place(fields_ref, modal_ref, out_ref, force_ref, held, force, in_sem, out_sem):
     count = fields_ref.shape[0]
-    pieces = [(fields_ref.at[f], held.at[f], out_ref.at[f]) for f in range(count)]
+    half = fields_ref.shape[1] // 2
+    places = [(f, pl.ds(part * half, half)) for f in range(count) for part in range(2)]
+    pieces = [(fields_ref.at[at], held.at[at], out_ref.at[at]) for at in places]
     pieces += [(modal_ref, force, force_ref)]
     comes = [
         pltpu.make_async_copy(src, mid, in_sem.at[i]) for i, (src, mid, _) in enumerate(pieces)
@@ -648,7 +653,7 @@
             pltpu.VMEM((2, 1, 128), f32),
             pltpu.VMEM((first_hop, 1, 128), f32),
             pltpu.VMEM((second_hop, 1, 128), f32),
-            dma((8 + PARTS,)),
+            dma((8 + 2 * PARTS,)),
             dma((4 + 8 * PARTS,)),
             dma((4 + 8 * PARTS,)),
             dma((1,)),
@@ -676,8 +681,8 @@
         scratch_shapes=[
             pltpu.VMEM(fields.shape, f32),
             pltpu.VMEM((1, n_modes), f32),
-            dma((FIELDS + 1,)),
-            dma((FIELDS + 1,)),
+            dma((2 * FIELDS + 1,)),
+            dma((2 * FIELDS + 1,)),
         ],
         compiler_params=pltpu.CompilerParams(vmem_limit_bytes=63 * 1024 * 1024),
         name="place_results",

time: 32.4 us -> 32.6 us (level)
  no operation moved by 1% of the time
where the time goes in v7:
time: 32.6 us; the launch traced here: 32.4 us
  Pallas kernels  31.8 us (98%)
  between operations  0.64 us (2%)
    pallas_call x1, Pallas kernels, on_device(): pl.pallas_call(functools.partial(kernel, sizes), out_shape=(jax.ShapeDtyp...  29.5 us
    pallas_call x1, Pallas kernels, on_device(): pl.pallas_call(place, out_shape=(jax.ShapeDtypeStruct(fields.shape, f32),...  2.23 us

profile of v7, /device:TPU:0, one launch (start us, length us, event | category | flops | bytes accessed | tf_op | source)
XLA Modules:
  0.0 32.4 jit_solution(7201736473929573671)
XLA Ops:
  0.6 29.5 %wind_steps.1 = (f32[5,32,16,128]{3,2,1,0:T(8,128)}, f32[1,32]{1,0:T(1,128)}) custom-call(f32[5,32,16,128]{3,2,1,0:T(8,128)} %fields_ref.1, f32[32,16,128]{2,1,0:T(8,128)} %solid_ref.1, f32[5,16,256]{2,1,0:T(8,128)} %bitcast.5, s32[1,16]{1,0:T(1,128)} %bitcast.6, s32[1,1,1,2048]{3,2,1,0:T(1,128)} %cells_ref.1, f32[1,4,3,1,2048]{4,3,2,1,0:T(1,128)} %bitcast.4, ...), custom_call_target="tpu_custom_call" | custom-call | tf_op jit(solution)/shard_map/wind_steps/pallas_call | solution.py:620
  30.2 2.2 %place_results.1 = (f32[5,32,16,128]{3,2,1,0:T(8,128)}, f32[1,32]{1,0:T(1,128)}) custom-call(f32[5,32,16,128]{3,2,1,0:T(8,128)} %get-tuple-element.6.fields_ref, f32[1,32]{1,0:T(1,128)} %get-tuple-element.7.modal_ref), custom_call_target="tpu_custom_call" | custom-call | tf_op jit(solution)/shard_map/place_results/pallas_call | solution.py:673
